TPU v7x, 128 devices: a whole 4x4x4 slice. The times are simulated.
128 devices in a mesh: section: 4 (over y_lo, core), seq: 32 (over z, y_hi, x).
Axes of the slice: x: 4, y: 4 (y_hi: 2, y_lo: 2; y = y_hi * 2 + y_lo), z: 4, core: 2. Of those that a mesh axis runs over, the one named last changes fastest.
Arguments:
- hidden_in: bfloat16 [4, 4096, 8192], P('section', 'seq'), may hold values from -64 to 64
- saved_hidden: bfloat16 [4, 4096, 8192], P('section', 'seq'), may hold values from -64 to 64
- grad_in: bfloat16 [4, 4096, 8192], P('section', 'seq'), may hold values from -6 to 6
- norm_gain: float32 [4, 8192], P('section'), may hold values from 0.25 to 1.75
- w_query: bfloat16 [4, 8192, 512], P('section', 'seq'), may hold values from -1 to 1
- w_key: bfloat16 [4, 8192, 128], P('section', 'seq'), may hold values from -1 to 1
- w_value: bfloat16 [4, 8192, 128], P('section', 'seq'), may hold values from -0.0625 to 0.0625
- w_out: bfloat16 [4, 512, 8192], P('section', 'seq'), may hold values from -0.25 to 0.25
- head: float32 [8192], replicated, may hold values from -0.0625 to 0.0625
- block_table: int32 [16], replicated, may hold values from 0 to 15, each once
- resp_lengths: int32 [8], replicated, may hold values from 1 to 256, 1536 in all
- pairs: int32 [28, 2], replicated, may hold values from 0 to 7, as said below
Outputs:
- next_hidden: bfloat16 [4, 4096, 8192], P('section', 'seq')
- prev_grad: bfloat16 [4, 4096, 8192], P('section', 'seq')
Inputs may be any that keep to these rules, and one draw needn't show every extreme that they name: `block_table`: each of the 16 prompt blocks appears once. `resp_lengths`: the longest response fills all 256 slots. `pairs`: each unordered pair of two different responses appears exactly once; the first entry is the preferred response.
All inputs are finite; a program needn't handle non-finite values.
Results may differ from a plain program's by a relative error of at most 0.04.
Values may be sent and summed in bfloat16 or wider, within the bound.
A program may use at most 128 MiB of HBM per device.

v0:
```python
from functools import partial

import jax
import jax.numpy as jnp
from jax import lax
from jax.sharding import PartitionSpec as P

HD = 128
RESP = 8
BLK = 128


EPSILON = 1e-05
ROPE_BASE = 500000.0
LOSS_SCALE = 1024.0
NEGATIVE = -1e30


def from_behind(value, axis, by):
    size = lax.axis_size(axis)
    pairs = [(i, i + by) for i in range(size) if 0 <= i + by < size]
    return lax.ppermute(value, axis, pairs)


def describe(indices, block_table, resp_lengths, prompt_len, answer_len):
    prompt_blocks = prompt_len // BLK
    in_prompt = indices < prompt_len
    block_of = jnp.clip(indices // BLK, 0, prompt_blocks - 1)
    table_hit = block_of[:, None] == jnp.arange(prompt_blocks, dtype=jnp.int32)[None, :]
    logical = jnp.sum(jnp.where(table_hit, block_table[None, :], 0), axis=1)
    offset = jnp.maximum(indices - prompt_len, 0)
    answer = jnp.clip(offset // answer_len, 0, RESP - 1)
    within = offset % answer_len
    answer_hit = answer[:, None] == jnp.arange(RESP, dtype=jnp.int32)[None, :]
    length = jnp.sum(jnp.where(answer_hit, resp_lengths[None, :], 0), axis=1)
    position = jnp.where(in_prompt, logical * BLK + indices % BLK, prompt_len + within)
    segment = jnp.where(in_prompt, -1, answer)
    usable = jnp.logical_or(in_prompt, within < length)
    return (position, segment, usable)


def visible(query_info, key_info):
    query_pos, query_seg, _ = query_info
    key_pos, key_seg, key_use = key_info
    causal = key_pos[None, :] <= query_pos[:, None]
    from_prompt = jnp.logical_and(
        key_seg[None, :] < 0, jnp.logical_or(query_seg[:, None] >= 0, causal)
    )
    same_answer = jnp.logical_and(key_seg[None, :] == query_seg[:, None], causal)
    return jnp.logical_and(key_use[None, :], jnp.logical_or(from_prompt, same_answer))


def rotate(values, position, direction):
    half_width = values.shape[-1] // 2
    frequency = ROPE_BASE ** (-2.0 * jnp.arange(half_width, dtype=jnp.float32) / values.shape[-1])
    angles = position.astype(jnp.float32)[:, None] * frequency[None, :]
    cosine = jnp.cos(angles)[:, None, :]
    sine_part = direction * jnp.sin(angles)[:, None, :]
    lower_half = values[..., :half_width]
    upper_half = values[..., half_width:]
    return jnp.concatenate(
        [
            lower_half * cosine - upper_half * sine_part,
            upper_half * cosine + lower_half * sine_part,
        ],
        axis=-1,
    )


def normalize(hidden, gain_row):
    widened = hidden.astype(jnp.float32)
    inv_rms = lax.rsqrt(jnp.mean(widened * widened, axis=1, keepdims=True) + EPSILON)
    return (inv_rms, (widened * inv_rms * gain_row[None, :]).astype(jnp.bfloat16))


def sweep(update, running, shard_rows):
    row_total = shard_rows.shape[0]
    block_rows = 512
    block_count = row_total // block_rows
    stacked = shard_rows.reshape(block_count, block_rows, shard_rows.shape[1])
    starts = jnp.arange(block_count, dtype=jnp.int32) * block_rows

    def advance(current, element):
        return (update(current, element[0], element[1]), None)

    running, _ = lax.scan(advance, running, (stacked, starts))
    return running


def forward_update(running, key_block, first_key, queries, query_info, describe_keys):
    key_info = describe_keys(first_key + jnp.arange(key_block.shape[0], dtype=jnp.int32))
    allowed = visible(query_info, key_info)[None]
    running_max, denominator, weighted = running
    scores = jnp.einsum(
        "qhd,kd->hqk", queries, key_block[:, :HD], preferred_element_type=jnp.float32
    ) * HD ** (-0.5)
    scores = jnp.where(allowed, scores, NEGATIVE)
    new_max = jnp.maximum(running_max, jnp.max(scores, axis=2))
    weights = jnp.where(allowed, jnp.exp(scores - new_max[:, :, None]), 0.0)
    factor = jnp.exp(running_max - new_max)
    denominator = denominator * factor + jnp.sum(weights, axis=2)
    weighted = weighted * factor[:, :, None] + jnp.einsum(
        "hqk,kd->hqd",
        weights.astype(jnp.bfloat16),
        key_block[:, HD:],
        preferred_element_type=jnp.float32,
    )
    return (new_max, denominator, weighted)


def backward_update(
    running,
    key_block,
    first_key,
    queries,
    query_info,
    describe_keys,
    d_heads,
    row_dots,
    row_max,
    denominator,
):
    block_rows = key_block.shape[0]
    key_info = describe_keys(first_key + jnp.arange(block_rows, dtype=jnp.int32))
    allowed = visible(query_info, key_info)[None]
    d_query, dkv_whole = running
    key_rows = key_block[:, :HD]
    scores = jnp.einsum(
        "qhd,kd->hqk", queries, key_rows, preferred_element_type=jnp.float32
    ) * HD ** (-0.5)
    scores = jnp.where(allowed, scores, NEGATIVE)
    probs = jnp.where(allowed, jnp.exp(scores - row_max[:, :, None]) / denominator[:, :, None], 0.0)
    d_probs = jnp.einsum(
        "qhd,kd->hqk", d_heads, key_block[:, HD:], preferred_element_type=jnp.float32
    )
    d_scores = (probs * (d_probs - row_dots[:, :, None])).astype(jnp.bfloat16)
    d_query = d_query + jnp.einsum(
        "hqk,kd->qhd", d_scores, key_rows, preferred_element_type=jnp.float32
    ) * HD ** (-0.5)
    d_key = jnp.einsum(
        "hqk,qhd->kd", d_scores, queries, preferred_element_type=jnp.float32
    ) * HD ** (-0.5)
    d_value = jnp.einsum(
        "hqk,qhd->kd", probs.astype(jnp.bfloat16), d_heads, preferred_element_type=jnp.float32
    )
    previous = lax.dynamic_slice_in_dim(dkv_whole, first_key, block_rows, 0)
    dkv_whole = lax.dynamic_update_slice_in_dim(
        dkv_whole, previous + jnp.concatenate([d_key, d_value], axis=1), first_key, 0
    )
    return (d_query, dkv_whole)


def per_device(
    hidden_in,
    saved_hidden,
    grad_in,
    norm_gain,
    w_query,
    w_key,
    w_value,
    w_out,
    head,
    block_table,
    resp_lengths,
    pairs,
):
    row_count = hidden_in.shape[1]
    seq_count = lax.axis_size("seq")
    tokens_all = row_count * seq_count
    prompt_len = tokens_all // 2
    answer_len = prompt_len // RESP
    first_row = lax.axis_index("seq") * row_count
    describe_keys = partial(
        describe,
        block_table=block_table,
        resp_lengths=resp_lengths,
        prompt_len=prompt_len,
        answer_len=answer_len,
    )
    local_rows = first_row + jnp.arange(row_count, dtype=jnp.int32)
    query_info = describe_keys(local_rows)
    position = query_info[0]
    gain_row = norm_gain[0]

    def attend_forward(hidden, w_q, w_k, w_v):
        inv_rms, normed = normalize(hidden, gain_row)
        head_count = w_q.shape[1] // HD
        queries = rotate(
            jnp.dot(normed, w_q, preferred_element_type=jnp.float32).reshape(
                row_count, head_count, HD
            ),
            position,
            1.0,
        ).astype(jnp.bfloat16)
        key_part = rotate(
            jnp.dot(normed, w_k, preferred_element_type=jnp.float32)[:, None, :], position, 1.0
        )[:, 0, :]
        value_part = jnp.dot(normed, w_v, preferred_element_type=jnp.float32)
        pairs_kv = jnp.concatenate([key_part, value_part], axis=1).astype(jnp.bfloat16)
        initial = (
            jnp.full((head_count, row_count), NEGATIVE, jnp.float32),
            jnp.zeros((head_count, row_count), jnp.float32),
            jnp.zeros((head_count, row_count, HD), jnp.float32),
        )
        update = partial(
            forward_update, queries=queries, query_info=query_info, describe_keys=describe_keys
        )
        running = sweep(update, initial, lax.all_gather(pairs_kv, "seq", axis=0, tiled=True))
        running_max, denominator, weighted = running
        mixed = (
            jnp.transpose(weighted / denominator[:, :, None], (1, 0, 2))
            .reshape(row_count, head_count * HD)
            .astype(jnp.bfloat16)
        )
        return (inv_rms, queries, pairs_kv, mixed, running_max, denominator)

    w_q, w_k, w_v, w_o = (
        lax.all_gather(w_query[0], "seq", axis=0, tiled=True),
        lax.all_gather(w_key[0], "seq", axis=0, tiled=True),
        lax.all_gather(w_value[0], "seq", axis=0, tiled=True),
        lax.all_gather(w_out[0], "seq", axis=0, tiled=True),
    )
    forward_now = attend_forward(hidden_in[0], w_q, w_k, w_v)
    layer_out = (
        jnp.dot(forward_now[3], w_o, preferred_element_type=jnp.float32)
        + hidden_in[0].astype(jnp.float32)
    ).astype(jnp.bfloat16)
    next_hidden = from_behind(layer_out[None], "section", 1)
    output_wide = layer_out.astype(jnp.float32)
    inv_out = lax.rsqrt(jnp.mean(output_wide * output_wide, axis=1, keepdims=True) + EPSILON)
    head_row = head[None, :]
    row_scores = jnp.sum(output_wide * inv_out * head_row, axis=1)
    end_rows = prompt_len + jnp.arange(RESP, dtype=jnp.int32) * answer_len + resp_lengths - 1
    end_hits = end_rows[:, None] == local_rows[None, :]
    partial_rewards = jnp.sum(jnp.where(end_hits, row_scores[None, :], 0.0), axis=1)
    rewards = lax.psum(partial_rewards, "seq")
    answers = jnp.arange(RESP, dtype=jnp.int32)[None, :]
    chosen_hit = pairs[:, 0:1] == answers
    rejected_hit = pairs[:, 1:2] == answers
    margin = jnp.sum(jnp.where(rejected_hit, rewards[None, :], 0.0), axis=1) - jnp.sum(
        jnp.where(chosen_hit, rewards[None, :], 0.0), axis=1
    )
    pressure = jax.nn.sigmoid(margin) * (LOSS_SCALE / pairs.shape[0])
    reward_grad = jnp.sum(jnp.where(rejected_hit, pressure[:, None], 0.0), axis=0) - jnp.sum(
        jnp.where(chosen_hit, pressure[:, None], 0.0), axis=0
    )
    row_grad = jnp.sum(jnp.where(end_hits, reward_grad[:, None], 0.0), axis=0)
    slope = inv_out * head_row - output_wide * inv_out**3 * jnp.mean(
        output_wide * head_row, axis=1, keepdims=True
    )
    last_cotangent = (row_grad[:, None] * slope).astype(jnp.bfloat16)
    is_last = lax.axis_index("section") == lax.axis_size("section") - 1
    source = jnp.where(is_last, hidden_in[0], saved_hidden[0])
    cotangent = jnp.where(is_last, last_cotangent, grad_in[0])
    inv_rms, queries, own_keys, mixed, row_max, denominator = attend_forward(source, w_q, w_k, w_v)
    head_count = queries.shape[1]
    d_mixed = jnp.dot(cotangent, w_o.T, preferred_element_type=jnp.float32).astype(jnp.bfloat16)
    d_heads = d_mixed.reshape(row_count, head_count, HD)
    row_dots = jnp.sum(
        d_heads.astype(jnp.float32) * mixed.reshape(row_count, head_count, HD).astype(jnp.float32),
        axis=2,
    ).T
    initial = (
        jnp.zeros((row_count, head_count, HD), jnp.float32),
        jnp.zeros((tokens_all, 2 * HD), jnp.float32),
    )
    update = partial(
        backward_update,
        queries=queries,
        query_info=query_info,
        describe_keys=describe_keys,
        d_heads=d_heads,
        row_dots=row_dots,
        row_max=row_max,
        denominator=denominator,
    )
    d_query, dkv_whole = sweep(update, initial, lax.all_gather(own_keys, "seq", axis=0, tiled=True))
    dkv_local = lax.psum_scatter(
        dkv_whole.astype(jnp.bfloat16), "seq", scatter_dimension=0, tiled=True
    ).astype(jnp.float32)
    back_query = (
        rotate(d_query, position, -1.0).reshape(row_count, head_count * HD).astype(jnp.bfloat16)
    )
    back_key = rotate(dkv_local[:, None, :HD], position, -1.0)[:, 0, :].astype(jnp.bfloat16)
    back_value = dkv_local[:, HD:].astype(jnp.bfloat16)
    d_normed = jnp.dot(back_query, w_q.T, preferred_element_type=jnp.float32)
    d_normed = d_normed + jnp.dot(back_key, w_k.T, preferred_element_type=jnp.float32)
    d_normed = d_normed + jnp.dot(back_value, w_v.T, preferred_element_type=jnp.float32)
    scaled_grad = d_normed * gain_row[None, :]
    widened = source.astype(jnp.float32)
    section_grad = (
        cotangent.astype(jnp.float32)
        + inv_rms * scaled_grad
        - widened * inv_rms**3 * jnp.mean(scaled_grad * widened, axis=1, keepdims=True)
    )
    prev_grad = from_behind(section_grad.astype(jnp.bfloat16)[None], "section", -1)
    return (next_hidden, prev_grad)


def solution(mesh):
    in_specs = (
        P("section", "seq", None),
        P("section", "seq", None),
        P("section", "seq", None),
        P("section", None),
        P("section", "seq", None),
        P("section", "seq", None),
        P("section", "seq", None),
        P("section", "seq", None),
        P(),
        P(),
        P(),
        P(),
    )
    out_specs = (P("section", "seq", None), P("section", "seq", None))
    return jax.shard_map(
        per_device, mesh=mesh, in_specs=in_specs, out_specs=out_specs, check_vma=False
    )
```

profile of v0, /device:TPU:1, one launch (start us, length us, event | category | flops | bytes accessed | tf_op | source)
XLA Modules:
  0.0 1068.6 jit_solution(6604533174899782345)
XLA Ops:
  9.5 4.2 fusion.105
  14.4 69.4 %all-gather.15.cloned.1.call-done = bf16[1,8192,128]{2,1,0:T(8,128)(2,1)} async-done(((bf16[1,256,128]{2,1,0:T(8,128)(2,1)}), bf16[1,8192,128]{2,1,0:T(8,128)(2,1)}) %all-gather.15.cloned.1.call-update) | async-done | bytes 2097168 | tf_op jit(solution)/shard_map/all_gather | solution.py:219
  83.8 3.5 fusion.147
  88.7 65.9 %all-gather.17.cloned.1.call-done = bf16[1,8192,128]{2,1,0:T(8,128)(2,1)} async-done(((bf16[1,256,128]{2,1,0:T(8,128)(2,1)}), bf16[1,8192,128]{2,1,0:T(8,128)(2,1)}) %all-gather.17.cloned.1.call-update) | async-done | bytes 2097168 | tf_op jit(solution)/shard_map/all_gather | solution.py:220
  154.5 3.3 fusion.153
  161.2 2.7 fusion.156
  164.8 60.3 %all-gather.11.cloned.1.call-done = bf16[4096,256]{0,1:T(8,128)(2,1)} async-done(((bf16[128,256]{0,1:T(8,128)(2,1)}), bf16[4096,256]{0,1:T(8,128)(2,1)}) %all-gather.11.cloned.1.call-update) | async-done | bytes 2097168 | tf_op jit(solution)/shard_map/all_gather | solution.py:208
  225.1 4.1 copy.89
  229.2 102.8 %all-gather.19.cloned.1.call-done = bf16[1,8192,512]{2,1,0:T(8,128)(2,1)} async-done(((bf16[1,256,512]{2,1,0:T(8,128)(2,1)}), bf16[1,8192,512]{2,1,0:T(8,128)(2,1)}) %all-gather.19.cloned.1.call-update) | async-done | bytes 8388624 | tf_op jit(solution)/shard_map/all_gather | solution.py:218
  332.0 12.0 %copy.72 = bf16[512,8192]{1,0:T(8,128)(2,1)} copy(bf16[512,8192]{0,1:T(8,128)(2,1)} %bitcast.271) | data formatting | bytes 16777216 | tf_op jit(solution)/shard_map/dot_general | solution.py:189
  344.0 6.0 fusion.124
  350.5 2.4 fusion.128
  353.2 61.0 %while.52 = (s32[]{:T(128)}, f32[4,128]{1,0:T(4,128)S(1)}, f32[4,128]{1,0:T(4,128)S(1)}, f32[4,128,128]{2,1,0:T(8,128)S(1)}, s32[8]{0:T(128)}, /*index=5*/s32[8]...) while((s32[]{:T(128)}, f32[4,128]{1,0:T(4,128)S(1)}, ...), condition=%wide.region_7.8_spmd.clone, body=%wide.region_2.7_spmd.clone.sunk | while | flops 137322624 | bytes 4911125 | solution.py:86
  414.3 22.5 %all-gather.21.cloned.1.call-done = bf16[1,512,8192]{2,1,0:T(8,128)(2,1)} async-done(((bf16[1,16,8192]{2,1,0:T(8,128)(2,1)}), bf16[1,512,8192]{2,1,0:T(8,128)(2,1)}) %all-gather.21.cloned.1.call-update) | async-done | bytes 8388624 | tf_op jit(solution)/shard_map/all_gather | solution.py:221
  436.9 5.9 fusion.114
  444.6 61.2 %all-gather.13.cloned.1.call-done = bf16[4096,256]{0,1:T(8,128)(2,1)} async-done(((bf16[128,256]{0,1:T(8,128)(2,1)}), bf16[4096,256]{0,1:T(8,128)(2,1)}) %all-gather.13.cloned.1.call-update) | async-done | bytes 2097168 | tf_op jit(solution)/shard_map/all_gather | solution.py:277
  505.8 4.1 copy.93
  509.9 80.1 %psum.7 = f32[8]{0:T(128)S(1)} all-reduce(f32[8]{0:T(128)S(1)} %fusion.192), channel_id=1, replica_groups=mesh['section'=4,'seq'=32] {'seq'}, use_global_device_ids=true, to_apply=%region_11.12 | all-reduce | flops 8 | bytes 64 | tf_op jit(solution)/shard_map/psum | solution.py:236
  592.3 92.6 %while.53 = (s32[]{:T(128)}, f32[4,128]{1,0:T(4,128)S(1)}, f32[4,128]{1,0:T(4,128)}, f32[4,128,128]{2,1,0:T(8,128)}, s32[8]{0:T(128)}, /*index=5*/s32[8]{0:T(128...) while((s32[]{:T(128)}, f32[4,128]{1,0:T(4,128)S(1)}, ...), condition=%wide.region_24.25_spmd.clone, body=%wide.region_19.24_spmd.clone.sunk | while | flops 137322624 | bytes 4911125 | solution.py:86
  612.2 2.1 convolution_add_fusion.8
  623.9 2.1 convolution_add_fusion.8
  635.7 2.1 convolution_add_fusion.8
  647.5 2.1 convolution_add_fusion.8
  659.3 2.1 convolution_add_fusion.8
  671.1 2.1 convolution_add_fusion.8
  682.8 2.1 convolution_add_fusion.8
  684.9 7.0 fusion.144
  692.3 2.4 broadcast_in_dim.388
  694.8 122.4 %while.54 = (s32[]{:T(128)}, f32[128,4,128]{0,2,1:T(8,128)S(1)}, f32[4096,256]{0,1:T(8,128)}, bf16[8,512,256]{2,1,0:T(8,128)(2,1)}, s32[8]{0:T(128)}, /*index=5*...) while((s32[]{:T(128)}, f32[128,4,128]{0,2,1:T(8,128)S(1)}, ...), condition=%wide.region_29.30_spmd.clone, body=%wide.region_26.29_spmd.clone.sunk | while | flops 338974336 | bytes 9996381 | solution.py:86
  706.3 3.5 dynamic_update_slice.9
  721.7 3.5 dynamic_update_slice.9
  737.1 3.5 dynamic_update_slice.9
  752.5 3.5 dynamic_update_slice.9
  767.9 3.5 dynamic_update_slice.9
  783.3 3.5 dynamic_update_slice.9
  798.7 3.5 dynamic_update_slice.9
  814.0 2.8 dynamic_update_slice.9
  817.1 3.8 convert_element_type.160
  820.9 4.2 copy.91
  825.2 18.0 %collective-permute-start = (bf16[1,128,8192]{2,1,0:T(8,128)(2,1)S(1)}, bf16[1,128,8192]{2,1,0:T(8,128)(2,1)}, u32[]{:S(2)}, u32[]{:S(2)}) collective-permute-start(bf16[1,128,8192]{2,1,0:T(8,128)(2,1)S(1)} %bitcast.272), channel_id=1, source_target_pairs={{0,32},{32,64},{64,96},{1,33},{33,65},{65,97},{2,34},{34,66},{66,9... | collective-permute-start | bytes 6291464 | tf_op jit(solution)/shard_map/ppermute | solution.py:22
  843.3 8.2 fusion.92
  851.5 146.3 %reduce-scatter.4.cloned.1.call-done = bf16[128,256]{1,0:T(8,128)(2,1)} async-done(((bf16[4096,256]{1,0:T(8,128)(2,1)}), bf16[128,256]{1,0:T(8,128)(2,1)}) %reduce-scatter.4.cloned.1.call-update) | async-done | bytes 65552
  999.0 3.7 convolution_add_fusion.3
  1004.6 2.7 fusion.126
  1007.3 26.4 %collective-permute-start.1 = (bf16[1,128,8192]{2,1,0:T(8,128)(2,1)S(1)}, bf16[1,128,8192]{2,1,0:T(8,128)(2,1)S(1)}, u32[]{:S(2)}, u32[]{:S(2)}) collective-permute-start(bf16[1,128,8192]{2,1,0:T(8,128)(2,1)S(1)} %fusion.126), channel_id=1, source_target_pairs={{32,0},{64,32},{96,64},{33,1},{65,33},{97,65},{34,2},{66,34},{98,6... | collective-permute-start | bytes 6291464 | tf_op jit(solution)/shard_map/ppermute | solution.py:22
  1033.8 23.6 %collective-permute-done.1 = bf16[1,128,8192]{2,1,0:T(8,128)(2,1)S(1)} collective-permute-done((bf16[1,128,8192]{2,1,0:T(8,128)(2,1)S(1)}, bf16[1,128,8192]{2,1,0:T(8,128)(2,1)S(1)}, u32[]{:S(2)}, u32[]{:S(2)}) %collective-permute-start.1) | collective-permute-done | bytes 2097184 | tf_op jit(solution)/shard_map/ppermute | solution.py:22
  1057.3 3.1 copy.135
  1060.4 1.3 copy.136
  (556 shorter events, 232.5 us)
Async XLA Ops:
  7.2 76.6 %copy-start.18 = (f32[1,8192]{1,0:T(1,128)S(1)}, f32[1,8192]{1,0:T(1,128)}, u32[]{:S(2)}) copy-start(f32[1,8192]{1,0:T(1,128)} %param.21) | copy-start | bytes 98308
  7.2 76.6 %all-gather.15.cloned.1.call-start = ((), (), s32[]{:S(2)}) async-start(), calls=%async_computation.3 | async-start | bytes 2162688 | tf_op jit(solution)/shard_map/all_gather | solution.py:219
  7.9 146.6 %all-gather.17.cloned.1.call-start = ((), (), s32[]{:S(2)}) async-start(), calls=%async_computation.4 | async-start | bytes 2162688 | tf_op jit(solution)/shard_map/all_gather | solution.py:220
  8.7 216.4 %all-gather.11.cloned.1.call-start = ((), (), s32[]{:S(2)}) async-start(), calls=%async_computation.1 | async-start | bytes 2162688 | tf_op jit(solution)/shard_map/all_gather | solution.py:208
  8.7 151.6 %copy-start.22 = (f32[64]{0:T(128)}, f32[64]{0:T(128)S(1)}, u32[]{:S(2)}) copy-start(f32[64]{0:T(128)S(1)} %multiply_power_fusion) | copy-start | bytes 772
  13.7 330.3 %copy-start = (bf16[1,128,8192]{2,1,0:T(8,128)(2,1)}, bf16[1,128,8192]{2,1,0:T(8,128)(2,1)S(1)}, u32[]{:S(2)}) copy-start(bf16[1,128,8192]{2,1,0:T(8,128)(2,1)S(1)} %get-tuple-element.966) | copy-start | bytes 6291460
  14.4 329.6 %copy-start.29 = (f32[128]{0:T(128)}, f32[128]{0:T(128)S(1)}, u32[]{:S(2)}) copy-start(f32[128]{0:T(128)S(1)} %get-tuple-element.1002) | copy-start | bytes 1540
  14.4 146.0 %copy-start.20 = (f32[128]{0:T(128)}, f32[128]{0:T(128)S(1)}, u32[]{:S(2)}) copy-start(f32[128]{0:T(128)S(1)} %get-tuple-element.967) | copy-start | bytes 1540
  83.8 3.5 copy-start.9
  88.4 71.9 %copy-start.15 = (s32[8]{0:T(128)S(1)}, s32[8]{0:T(128)}, u32[]{:S(2)}) copy-start(s32[8]{0:T(128)} %param.28) | copy-start | bytes 100
  88.4 71.9 %copy-start.27 = (s32[28,2]{0,1:T(2,128)S(1)}, s32[28,2]{0,1:T(2,128)}, u32[]{:S(2)}) copy-start(s32[28,2]{0,1:T(2,128)} %param.29) | copy-start | bytes 676
  158.5 173.5 %all-gather.19.cloned.1.call-start = ((), (), s32[]{:S(2)}) async-start(), calls=%async_computation.5 | async-start | bytes 8650752 | tf_op jit(solution)/shard_map/all_gather | solution.py:218
  159.1 277.7 %all-gather.21.cloned.1.call-start = ((), (), s32[]{:S(2)}) async-start(), calls=%async_computation.6 | async-start | bytes 8650752 | tf_op jit(solution)/shard_map/all_gather | solution.py:221
  159.7 346.1 %all-gather.13.cloned.1.call-start = ((), (), s32[]{:S(2)}) async-start(), calls=%async_computation.2 | async-start | bytes 2162688 | tf_op jit(solution)/shard_map/all_gather | solution.py:277
  164.5 833.3 %reduce-scatter.4.cloned.1.call-start = ((), (), s32[]{:S(2)}) async-start(), calls=%async_computation.7 | async-start | bytes 2162688
  344.0 6.0 copy-start.5
  344.0 6.5 copy-start.6
  436.9 6.5 copy-start.13
  442.7 242.2 %copy-start.2 = (bf16[128,8192]{1,0:T(8,128)(2,1)}, bf16[128,8192]{1,0:T(8,128)(2,1)S(1)}, u32[]{:S(2)}) copy-start(bf16[128,8192]{1,0:T(8,128)(2,1)S(1)} %get-tuple-element.1006) | copy-start | bytes 6291460
  443.3 149.0 %copy-start.24 = (f32[128]{0:T(128)}, f32[128]{0:T(128)S(1)}, u32[]{:S(2)}) copy-start(f32[128]{0:T(128)S(1)} %get-tuple-element.1004) | copy-start | bytes 1540
  591.5 0.8 copy-start.7
  684.9 7.2 copy-start.12
  684.9 7.2 copy-start.16
  691.9 2.9 copy-start.4
  691.9 2.9 copy-start.8
  820.9 4.3 copy-start.3
  820.9 22.3 %copy-start.14 = (f32[128,64]{0,1:T(8,128)S(1)}, f32[128,64]{0,1:T(8,128)}, u32[]{:S(2)}) copy-start(f32[128,64]{0,1:T(8,128)} %get-tuple-element.994) | copy-start | bytes 98308
  825.2 208.6 %collective-permute-start = (bf16[1,128,8192]{2,1,0:T(8,128)(2,1)S(1)}, bf16[1,128,8192]{2,1,0:T(8,128)(2,1)}, u32[]{:S(2)}, u32[]{:S(2)}) collective-permute-start(bf16[1,128,8192]{2,1,0:T(8,128)(2,1)S(1)} %bitcast.272), channel_id=1, source_target_pairs={{0,32},{32,64},{64,96},{1,33},{33,65},{65,97},{2,34},{34,66},{66,9... | collective-permute-start | bytes 6291464 | tf_op jit(solution)/shard_map/ppermute | solution.py:22
  843.3 155.4 %copy-start.21 = (f32[128]{0:T(128)S(1)}, f32[128]{0:T(128)}, u32[]{:S(2)}) copy-start(f32[128]{0:T(128)} %copy-done.20) | copy-start | bytes 1540
  843.3 155.4 %copy-start.23 = (f32[64]{0:T(128)S(1)}, f32[64]{0:T(128)}, u32[]{:S(2)}) copy-start(f32[64]{0:T(128)} %copy-done.22) | copy-start | bytes 772
  998.9 3.7 copy-start.1
  999.0 4.1 copy-start.10
  999.0 4.0 copy-start.17
  999.0 4.0 copy-start.19
  1003.0 1.6 copy-start.11
  1003.0 1.6 copy-start.25
  1003.0 1.6 copy-start.26
  1003.0 1.6 copy-start.28
  1003.0 1.6 copy-start.30
  1003.1 1.6 copy-start.31
  1003.1 1.6 copy-start.32
  1007.3 50.0 %collective-permute-start.1 = (bf16[1,128,8192]{2,1,0:T(8,128)(2,1)S(1)}, bf16[1,128,8192]{2,1,0:T(8,128)(2,1)S(1)}, u32[]{:S(2)}, u32[]{:S(2)}) collective-permute-start(bf16[1,128,8192]{2,1,0:T(8,128)(2,1)S(1)} %fusion.126), channel_id=1, source_target_pairs={{32,0},{64,32},{96,64},{33,1},{65,33},{97,65},{34,2},{66,34},{98,6... | collective-permute-start | bytes 6291464 | tf_op jit(solution)/shard_map/ppermute | solution.py:22
Sparse Core Ops, SparseCore 0:
  11.0 72.7 all-gather.14
  86.8 67.6 all-gather.16
  158.6 66.3 all-gather.10
  227.9 103.9 all-gather.18
  334.8 101.9 all-gather.20
  439.5 66.3 all-gather.12
  825.3 172.4 reduce-scatter.3
where the time goes:
time: 1070 us
  waiting for transfers between devices  555 us (52%)
  other arithmetic  152 us (14%)
  local copies, waits for them, and re-layouts  115 us (11%)
  matrix products  88.6 us (8%)
  blocking collectives  80.1 us (7%)
  starting transfers between devices  44.9 us (4%)
  loops' own time  18.5 us (2%)
  between operations  14.8 us (1%)
    unnamed x8, waiting for transfers between devices  149 us
    all_gather x1, waiting for transfers between devices, per_device(): lax.all_gather(w_query[0], 'seq', axis=0, tiled=True)  103 us
    psum x1, blocking collectives, per_device(): rewards = lax.psum(partial_rewards, 'seq')  80.1 us
    all_gather x1, waiting for transfers between devices, per_device(): lax.all_gather(w_key[0], 'seq', axis=0, tiled=True)  69.4 us
    all_gather x1, waiting for transfers between devices, per_device(): lax.all_gather(w_value[0], 'seq', axis=0, tiled=True)  65.9 us
    all_gather x1, waiting for transfers between devices, per_device(): lax.all_gather(own_keys, 'seq', axis=0, tiled=True)  61.2 us
    all_gather x1, waiting for transfers between devices, attend_forward(): lax.all_gather(pairs_kv, 'seq', axis=0, tiled=True)  60.3 us
    ppermute x2, starting transfers between devices, from_behind(): return lax.ppermute(value, axis, pairs)  44.5 us
  transfers between devices with their start and end apart: 9, of which 8 were waited for; matrix products, arithmetic and copies ran while one was open for 12% of the time, Pallas kernels for 0%

commit v1 on v0

v1 whole, which is shorter than its diff:
```python
import functools
import math

import jax
import jax.numpy as jnp
from jax import lax
from jax.experimental import pallas as pl
from jax.experimental.pallas import tpu as pltpu
from jax.sharding import PartitionSpec as P

HD = 128
QH = 4
RESP = 8
BLK = 128
D = 8192
ROWS = 128
SEQ = 32
PBLK = 16
PROMPT = 2048
RLEN = 256
QKV = 768
EPSILON = 1e-05
ROPE_BASE = 500000.0
LOSS_SCALE = 1024.0
NEGATIVE = -1e30
FAR = 1 << 30
SCALE = HD**-0.5
LOG2 = SCALE / math.log(2.0)
OUT_COLS = 1024
OUT_STEPS = D // OUT_COLS
BACK_COLS = 512
BACK_STEPS = D // BACK_COLS

f32 = jnp.float32
bf16 = jnp.bfloat16

ORDER = ((0, 0), (1, 0), (0, 1), (0, 3), (1, 1), (1, 3), (0, 2), (1, 2))


def nt(a, b):
    return lax.dot_general(a, b, (((1,), (1,)), ((), ())), preferred_element_type=f32)


def tn(a, b):
    return lax.dot_general(a, b, (((0,), (0,)), ((), ())), preferred_element_type=f32)


def nn(a, b):
    return jnp.dot(a, b, preferred_element_type=f32)


class Place:
    def __init__(self):
        self.seq = lax.axis_index("seq")
        self.z = self.seq // 8
        self.y = (self.seq // 4) % 2
        self.x = self.seq % 4

    def at(self, dz=0, dy=0, dx=0):
        return ((self.z + dz) % 4) * 8 + ((self.y + dy) % 2) * 4 + (self.x + dx) % 4


class Gather:
    def __init__(self, place, view, send_sems, recv_sems, only=None):
        self.place, self.view, self.only = place, view, only
        self.send_sems, self.recv_sems = send_sems, recv_sems
        self.sent = []
        self.slots = {}
        for part in range(2):
            for dy, da in ORDER:
                for db in (0, 1, 3, 2):
                    for sub in (0, 1) if (da == 2 and db == 0) or db == 2 else (0,):
                        if (dy, da, db) != (0, 0, 0):
                            self.slots[(part, dy, da, db, sub)] = len(self.slots)

    def origin(self, part, dy, da, db):
        dx, dz = (da, db) if part == 0 else (db, da)
        return self.place.at(dz, dy, dx)

    def guard(self, part, da, db, action):
        if self.only is None:
            action()
        else:
            dz = db if part == 0 else da
            pl.when(self.only((self.place.z + dz) % 4))(action)

    def piece(self, part, dy, da, db, sub):
        return self.view(self.origin(part, dy, da, db), part, sub)

    def push(self, part, dy, da, db, axis, step, sub=None):
        if axis == "y":
            target, key = self.place.at(0, 1, 0), (part, 1 - dy, da, db, 0)
        else:
            along_x = (axis == "a") == (part == 0)
            target = self.place.at(0, 0, step) if along_x else self.place.at(step, 0, 0)
            if axis == "a":
                key = (part, dy, (da - step) % 4, db, sub or 0)
            else:
                key = (part, dy, da, (db - step) % 4, sub or 0)
        ref = self.piece(part, dy, da, db, sub)
        number = len(self.sent)
        copy = pltpu.make_async_remote_copy(
            src_ref=ref,
            dst_ref=ref,
            send_sem=self.send_sems.at[number] if self.only else self.send_sems.at[0],
            recv_sem=self.recv_sems.at[self.slots[key]],
            device_id={"seq": target},
            device_id_type=pl.DeviceIdType.MESH,
        )
        self.sent.append((part, da, db, copy))
        self.guard(part, da, db, copy.start)

    def take(self, part, dy, da, db, sub=None):
        ref = self.piece(part, dy, da, db, sub)
        copy = pltpu.make_async_remote_copy(
            src_ref=ref,
            dst_ref=ref,
            send_sem=self.send_sems.at[0],
            recv_sem=self.recv_sems.at[self.slots[(part, dy, da, db, sub or 0)]],
            device_id={"seq": self.place.at(0, 1, 0)},
            device_id_type=pl.DeviceIdType.MESH,
        )
        self.guard(part, da, db, copy.wait_recv)

    def begin(self):
        for part in range(2):
            self.push(part, 0, 0, 0, "y", 1)
        for part in range(2):
            for axis in ("a", "b"):
                for step in (1, -1):
                    self.push(part, 0, 0, 0, axis, step)

    def first(self, part, k):
        dy, da = ORDER[k]
        if (dy, da) == (0, 0):
            return
        if da == 2:
            self.take(part, dy, 2, 0, 0)
            self.take(part, dy, 2, 0, 1)
        else:
            self.take(part, dy, da, 0)
            if da == 0:
                self.push(part, dy, 0, 0, "a", 1)
                self.push(part, dy, 0, 0, "a", -1)
            elif da == 1:
                self.push(part, dy, 1, 0, "a", -1, 1)
            else:
                self.push(part, dy, 3, 0, "a", 1, 0)
        self.push(part, dy, da, 0, "b", 1)
        self.push(part, dy, da, 0, "b", -1)

    def second(self, part, k):
        dy, da = ORDER[k]
        self.take(part, dy, da, 1)
        self.push(part, dy, da, 1, "b", -1, 1)
        self.take(part, dy, da, 3)
        self.push(part, dy, da, 3, "b", 1, 0)

    def third(self, part, k):
        dy, da = ORDER[k]
        self.take(part, dy, da, 2, 0)
        self.take(part, dy, da, 2, 1)

    def steps(self):
        count = len(ORDER)
        for k in range(count + 2):
            here = []
            for part in range(2):
                if k < count:
                    self.first(part, k)
            for part in range(2):
                if 1 <= k <= count:
                    self.second(part, k - 1)
                    dy, da = ORDER[k - 1]
                    here += [(part, self.origin(part, dy, da, db)) for db in (0, 1, 3)]
                if k >= 2:
                    self.third(part, k - 2)
                    dy, da = ORDER[k - 2]
                    here.append((part, self.origin(part, dy, da, 2)))
            yield here

    def finish(self, whole=None):
        if self.only is None:
            pltpu.make_async_remote_copy(
                src_ref=whole,
                dst_ref=whole,
                send_sem=self.send_sems.at[0],
                recv_sem=self.recv_sems.at[0],
                device_id={"seq": self.place.at(0, 1, 0)},
                device_id_type=pl.DeviceIdType.MESH,
            ).wait_send()
        else:
            for part, da, db, copy in self.sent:
                self.guard(part, da, db, copy.wait_send)


def layer_kernel(
    scalars,
    hid_hbm,
    sav_hbm,
    gin_hbm,
    wq_hbm,
    wk_hbm,
    wv_hbm,
    wo_hbm,
    gain,
    head,
    cosine,
    sine,
    sign,
    nh_hbm,
    pg_hbm,
    hid,
    src,
    cot,
    xn,
    wqkv,
    wout,
    acc,
    queries,
    kv,
    mixed,
    layer_out,
    dheads,
    dkv,
    landed,
    tile,
    tiles,
    back,
    grad,
    zero,
    load_sems,
    wqkv_send,
    wqkv_recv,
    wout_send,
    wout_recv,
    kv_send,
    kv_recv,
    pair_sems,
    rs_send,
    rs_recv,
    tile_send,
    tile_recv,
    next_send,
    next_recv,
    prev_send,
    prev_recv,
    zero_sems,
):
    place = Place()
    seq = place.seq
    section = lax.axis_index("section")
    is_last = section == 3
    parity = seq % 2
    partner = seq + 1 - 2 * parity
    in_prompt = seq < PBLK

    def other(index):
        return {"seq": index}

    loads = [
        pltpu.make_async_copy(wq_hbm, wqkv.at[seq, :, pl.ds(0, 512)], load_sems.at[0]),
        pltpu.make_async_copy(wk_hbm, wqkv.at[seq, :, pl.ds(512, 128)], load_sems.at[1]),
        pltpu.make_async_copy(wv_hbm, wqkv.at[seq, :, pl.ds(640, 128)], load_sems.at[2]),
        pltpu.make_async_copy(hid_hbm, hid, load_sems.at[3]),
        pltpu.make_async_copy(wo_hbm, wout.at[seq], load_sems.at[4]),
        pltpu.make_async_copy(gin_hbm, cot, load_sems.at[5]),
    ]
    for load in loads[:4]:
        load.start()
    saved_load = pltpu.make_async_copy(sav_hbm, src, load_sems.at[6])
    again_load = pltpu.make_async_copy(hid_hbm, src, load_sems.at[6])
    pl.when(jnp.logical_not(is_last))(saved_load.start)
    pl.when(is_last)(again_load.start)
    loads[4].start()
    loads[5].start()

    barrier = pltpu.get_barrier_semaphore()

    def greet(j, carry):
        pl.semaphore_signal(
            barrier, inc=1, device_id=other((seq + j) % SEQ), device_id_type=pl.DeviceIdType.MESH
        )
        return carry

    lax.fori_loop(1, SEQ, greet, 0)
    for step in (1, 3):
        pl.semaphore_signal(
            barrier,
            inc=1,
            device_id={"section": (section + step) % 4},
            device_id_type=pl.DeviceIdType.MESH,
        )
    for load in loads[:3]:
        load.wait()
    pl.semaphore_wait(barrier, SEQ - 1 + 2)

    def qkv_view(o, part, sub):
        if sub is None:
            return wqkv.at[o, pl.ds(part * 128, 128), :]
        return wqkv.at[o, pl.ds(part * 128 + sub * 64, 64), :]

    def out_view(o, part, sub):
        if sub is None:
            return wout.at[o, :, pl.ds(part * 4096, 4096)]
        return wout.at[o, :, pl.ds(part * 4096 + sub * 2048, 2048)]

    qkv_gather = Gather(place, qkv_view, wqkv_send, wqkv_recv)
    out_gather = Gather(place, out_view, wout_send, wout_recv)
    qkv_gather.begin()

    acc[...] = jnp.zeros_like(acc)
    zero[...] = jnp.zeros_like(zero)

    def inverse_rms(buf):
        def body(i, total):
            wide = buf[:, pl.ds(pl.multiple_of(i * 512, 512), 512)].astype(f32)
            wide = wide * wide
            return total + (
                (wide[:, :128] + wide[:, 128:256]) + (wide[:, 256:384] + wide[:, 384:])
            )

        total = lax.fori_loop(0, 16, body, jnp.zeros((ROWS, 128), f32))
        return lax.rsqrt(jnp.sum(total, axis=1, keepdims=True) * (1.0 / D) + EPSILON)

    def normalize(buf, row):
        inv = inverse_rms(buf)

        def body(i, carry):
            at = pl.ds(pl.multiple_of(i * 128, 128), 128)
            xn[i, pl.ds(row, ROWS), :] = (buf[:, at].astype(f32) * inv * gain[:, at]).astype(bf16)
            return carry

        lax.fori_loop(0, 64, body, 0)
        return inv

    loads[3].wait()
    normalize(hid, 0)
    saved_load.wait()
    inv_src = normalize(src, ROWS)
    loads[4].wait()
    loads[5].wait()

    for step, here in enumerate(qkv_gather.steps()):
        for part, o in here:
            acc[...] += nn(xn[o * 2 + part], wqkv[o, part * 128 : part * 128 + 128, :])

    cos, sin = cosine[...], sine[...]
    for t in range(2):
        row = slice(t * ROWS, (t + 1) * ROWS)
        for h in range(QH + 1):
            u = acc[row, h * HD : (h + 1) * HD]
            u = (u * cos + pltpu.roll(u, HD // 2, 1) * sin).astype(bf16)
            if h < QH:
                queries[t, h * HD : (h + 1) * HD, :] = u
            else:
                kv[PBLK + parity, :, t * 256 : t * 256 + 128] = u
        kv[PBLK + parity, :, t * 256 + 128 : t * 256 + 256] = acc[row, 640:768].astype(bf16)

    def keep_own():
        kv[seq] = kv[PBLK + parity]

    pl.when(in_prompt)(keep_own)
    own_kv = kv.at[PBLK + parity]
    pair_copy = pltpu.make_async_remote_copy(
        src_ref=own_kv,
        dst_ref=own_kv,
        send_sem=pair_sems.at[0],
        recv_sem=pair_sems.at[1],
        device_id=other(partner),
        device_id_type=pl.DeviceIdType.MESH,
    )

    def kv_view(o, part, sub):
        if sub is None:
            return kv.at[o, pl.ds(part * 64, 64), :]
        return kv.at[o, pl.ds(part * 64 + sub * 32, 32), :]

    kv_gather = Gather(place, kv_view, kv_send, kv_recv, only=lambda z: z < 2)
    kv_gather.begin()
    pair_copy.start()
    out_gather.begin()
    for _ in kv_gather.steps():
        pass
    pair_copy.wait_send()
    pltpu.make_async_remote_copy(
        src_ref=own_kv,
        dst_ref=kv.at[PBLK + 1 - parity],
        send_sem=pair_sems.at[0],
        recv_sem=pair_sems.at[1],
        device_id=other(partner),
        device_id_type=pl.DeviceIdType.MESH,
    ).wait_recv()
    kv_gather.finish()

    across = lax.broadcasted_iota(jnp.int32, (1, QH * ROWS), 1) % ROWS
    query_pos = scalars[19] + across
    down = lax.broadcasted_iota(jnp.int32, (2 * BLK, 1), 0)

    def allowed(c):
        key_pos = jnp.where(down < BLK, scalars[2 * c] + down, scalars[2 * c + 1] + (down - BLK))
        key_pos = jnp.where(key_pos < scalars[18], key_pos, FAR)
        return key_pos <= query_pos

    def keys_of(c, t):
        return kv[pl.ds(2 * c, 2), :, t * 256 : t * 256 + 128].reshape(2 * BLK, HD)

    def values_of(c, t):
        return kv[pl.ds(2 * c, 2), :, t * 256 + 128 : t * 256 + 256].reshape(2 * BLK, HD)

    out_steps = out_gather.steps()

    def attend(t):
        q = queries[t]

        def chunk(c, carry):
            row_max, total, weighted = carry
            scores = jnp.where(allowed(c), nt(keys_of(c, t), q), NEGATIVE)
            new_max = jnp.maximum(row_max, jnp.max(scores, axis=0, keepdims=True))
            weights = jnp.exp2((scores - new_max) * LOG2)
            factor = jnp.exp2((row_max - new_max) * LOG2)
            total = total * factor + jnp.sum(weights, axis=0, keepdims=True)
            weighted = weighted * factor + tn(values_of(c, t), weights.astype(bf16))
            return new_max, total, weighted

        carry = (
            jnp.full((1, QH * ROWS), NEGATIVE, f32),
            jnp.zeros((1, QH * ROWS), f32),
            jnp.zeros((HD, QH * ROWS), f32),
        )
        for start in (0, 3, 6):
            carry = lax.fori_loop(start, start + 3, chunk, carry)
            next(out_steps)
        row_max, total, weighted = carry
        weighted = weighted / total
        for h in range(QH):
            mixed[t, :, h * HD : (h + 1) * HD] = weighted[:, h * HD : (h + 1) * HD].T.astype(bf16)
        return row_max * LOG2 + jnp.log2(total)

    log_total = attend(1)
    attend(0)
    for _ in out_steps:
        pass

    mixed_now = mixed[0]
    next_copies = []
    squares = jnp.zeros((ROWS, 128), f32)
    products = jnp.zeros((ROWS, 128), f32)
    for c in range(OUT_STEPS):
        at = pl.ds(c * OUT_COLS, OUT_COLS)
        w = wout[:, :, at].reshape(QH * HD, OUT_COLS)
        y = (nn(mixed_now, w) + hid[:, at].astype(f32)).astype(bf16)
        layer_out[:, at] = y
        next_copies.append(
            pltpu.make_async_remote_copy(
                src_ref=layer_out.at[:, at],
                dst_ref=nh_hbm.at[0, :, at],
                send_sem=next_send.at[c],
                recv_sem=next_recv.at[c],
                device_id={"section": (section + 1) % 4},
                device_id_type=pl.DeviceIdType.MESH,
            )
        )
        pl.when(section < 3)(next_copies[-1].start)
        wide = y.astype(f32)
        scored = wide * head[:, at]
        wide = wide * wide
        for part in range(OUT_COLS // 128):
            squares += wide[:, part * 128 : part * 128 + 128]
            products += scored[:, part * 128 : part * 128 + 128]

    zero_next = [
        pltpu.make_async_copy(
            zero, nh_hbm.at[0, :, pl.ds(c * OUT_COLS, OUT_COLS)], zero_sems.at[c]
        )
        for c in range(OUT_STEPS)
    ]
    zero_prev = [
        pltpu.make_async_copy(
            zero, pg_hbm.at[0, :, pl.ds(c * OUT_COLS, OUT_COLS)], zero_sems.at[c]
        )
        for c in range(OUT_STEPS)
    ]

    def clear_next():
        for copy in zero_next:
            copy.start()

    def clear_prev():
        for copy in zero_prev:
            copy.start()

    pl.when(section == 0)(clear_next)
    pl.when(is_last)(clear_prev)

    def reward_rows():
        mean_square = jnp.sum(squares, axis=1, keepdims=True) * (1.0 / D)
        dots = jnp.sum(products, axis=1, keepdims=True)
        inv = lax.rsqrt(mean_square + EPSILON)
        rows = lax.broadcasted_iota(jnp.int32, (ROWS, 1), 0)
        hit = rows == scalars[20]
        reward = jnp.sum(jnp.where(hit, dots * inv, 0.0), axis=0, keepdims=True)
        tile[...] = jnp.broadcast_to(reward, (8, 128))
        me = seq - PBLK
        copies = []
        for j in range(1, PBLK):
            copies.append(
                pltpu.make_async_remote_copy(
                    src_ref=tile,
                    dst_ref=tiles.at[me],
                    send_sem=tile_send.at[j],
                    recv_sem=tile_recv.at[me],
                    device_id=other(PBLK + (me + j) % PBLK),
                    device_id_type=pl.DeviceIdType.MESH,
                )
            )
            copies[-1].start()
        tiles[me] = tile[...]
        for j in range(1, PBLK):
            source = (me + j) % PBLK
            pltpu.make_async_remote_copy(
                src_ref=tile,
                dst_ref=tiles.at[source],
                send_sem=tile_send.at[0],
                recv_sem=tile_recv.at[source],
                device_id=other(partner),
                device_id_type=pl.DeviceIdType.MESH,
            ).wait_recv()
        for copy in copies:
            copy.wait_send()
        mine = tiles[pl.ds(me // 2 * 2, 1), 0:1].reshape(1, 128) + tiles[
            pl.ds(me // 2 * 2 + 1, 1), 0:1
        ].reshape(1, 128)
        pull = jnp.zeros((1, 128), f32)
        for r in range(RESP):
            way = sign[r : r + 1, :]
            reward_r = tiles[2 * r, 0:1] + tiles[2 * r + 1, 0:1]
            pull += way / (1.0 + jnp.exp(way * (reward_r - mine)))
        pull = pull * (LOSS_SCALE / 28.0)
        row_grad = jnp.where(hit, jnp.sum(pull, axis=1, keepdims=True) * (1.0 / 128.0), 0.0)
        by_head = row_grad * inv
        by_out = row_grad * (inv * inv * inv) * (dots * (1.0 / D))

        def body(c, carry):
            at = pl.ds(pl.multiple_of(c * OUT_COLS, OUT_COLS), OUT_COLS)
            cot[:, at] = (by_head * head[:, at] - layer_out[:, at].astype(f32) * by_out).astype(
                bf16
            )
            return carry

        lax.fori_loop(0, OUT_STEPS, body, 0)

    def no_rewards():
        cot[...] = jnp.zeros_like(cot)

    pl.when(jnp.logical_and(is_last, jnp.logical_not(in_prompt)))(reward_rows)
    pl.when(jnp.logical_and(is_last, in_prompt))(no_rewards)

    def mix_back(c, total):
        at = pl.ds(pl.multiple_of(c * OUT_COLS, OUT_COLS), OUT_COLS)
        return total + nt(cot[:, at], wout[:, :, at].reshape(QH * HD, OUT_COLS))

    d_mixed = lax.fori_loop(0, OUT_STEPS, mix_back, jnp.zeros((ROWS, QH * HD), f32)).astype(bf16)
    dots = d_mixed.astype(f32) * mixed[1].astype(f32)
    row_dots = []
    for h in range(QH):
        dheads[h * HD : (h + 1) * HD, :] = d_mixed[:, h * HD : (h + 1) * HD]
        row_dots.append(jnp.sum(dots[:, h * HD : (h + 1) * HD].T, axis=0, keepdims=True))
    row_dots = jnp.concatenate(row_dots, axis=1)

    q = queries[1]
    dh = dheads[...]

    def attend_back(c, d_query):
        keys, values = keys_of(c, 1), values_of(c, 1)
        probs = jnp.exp2(jnp.where(allowed(c), nt(keys, q) * LOG2 - log_total, NEGATIVE))
        d_scores = (probs * (nt(values, dh) - row_dots)).astype(bf16)
        d_key = (nn(d_scores, q) * SCALE).astype(bf16)
        d_value = nn(probs.astype(bf16), dh).astype(bf16)
        dkv[pl.ds(2 * c, 2), :, 0:128] = d_key.reshape(2, BLK, HD)
        dkv[pl.ds(2 * c, 2), :, 128:256] = d_value.reshape(2, BLK, HD)
        return d_query + tn(keys, d_scores)

    def to_owner(owner):
        return pltpu.make_async_remote_copy(
            src_ref=dkv.at[owner],
            dst_ref=landed.at[seq],
            send_sem=rs_send.at[owner],
            recv_sem=rs_recv.at[seq],
            device_id=other(owner),
            device_id_type=pl.DeviceIdType.MESH,
        )

    def back_chunk(i, d_query):
        c = (i + seq) % 8
        d_query = attend_back(c, d_query)
        for half in range(2):
            owner = 2 * c + half
            pl.when(owner != seq)(to_owner(owner).start)
        return d_query

    d_query = attend_back(8, jnp.zeros((HD, QH * ROWS), f32))
    to_partner = pltpu.make_async_remote_copy(
        src_ref=dkv.at[PBLK + 1 - parity],
        dst_ref=landed.at[seq],
        send_sem=rs_send.at[PBLK],
        recv_sem=rs_recv.at[seq],
        device_id=other(partner),
        device_id_type=pl.DeviceIdType.MESH,
    )
    pl.when(jnp.logical_not(in_prompt))(to_partner.start)
    d_query = lax.fori_loop(0, 8, back_chunk, d_query) * SCALE

    for h in range(QH):
        u = d_query[:, h * HD : (h + 1) * HD].T
        back[:, h * HD : (h + 1) * HD] = (u * cos - pltpu.roll(u, HD // 2, 1) * sin).astype(bf16)

    def arrived(source):
        pltpu.make_async_remote_copy(
            src_ref=dkv.at[0],
            dst_ref=landed.at[source],
            send_sem=rs_send.at[0],
            recv_sem=rs_recv.at[source],
            device_id=other(partner),
            device_id_type=pl.DeviceIdType.MESH,
        ).wait_recv()

    def keep(total):
        u = total[:, :HD]
        back[:, 512:640] = (u * cos - pltpu.roll(u, HD // 2, 1) * sin).astype(bf16)
        back[:, 640:768] = total[:, HD:].astype(bf16)

    def sum_prompt():
        def body(j, total):
            source = (seq + j) % SEQ
            arrived(source)
            return total + landed[source].astype(f32)

        keep(lax.fori_loop(1, SEQ, body, dkv[seq].astype(f32)))

    def sum_answer():
        arrived(partner)
        keep(dkv[PBLK + parity].astype(f32) + landed[partner].astype(f32))

    pl.when(in_prompt)(sum_prompt)
    pl.when(jnp.logical_not(in_prompt))(sum_answer)

    back_all = back[...]
    along = jnp.sum(back_all.astype(f32) * acc[ROWS:, :], axis=1, keepdims=True)
    along = along * (inv_src * inv_src) * (1.0 / D)
    prev_copies = []
    for c in range(BACK_STEPS):
        at = pl.ds(c * BACK_COLS, BACK_COLS)
        w = wqkv[2 * c : 2 * c + 2].reshape(BACK_COLS, QKV)
        u = nt(back_all, w) * gain[:, at]
        grad[:, at] = (
            cot[:, at].astype(f32) + inv_src * u - src[:, at].astype(f32) * along
        ).astype(bf16)
        prev_copies.append(
            pltpu.make_async_remote_copy(
                src_ref=grad.at[:, at],
                dst_ref=pg_hbm.at[0, :, at],
                send_sem=prev_send.at[c],
                recv_sem=prev_recv.at[c],
                device_id={"section": (section + 3) % 4},
                device_id_type=pl.DeviceIdType.MESH,
            )
        )
        pl.when(section > 0)(prev_copies[-1].start)

    qkv_gather.finish(wqkv.at[pl.ds(0, SEQ - 1)])
    out_gather.finish(wout.at[pl.ds(0, SEQ - 1)])

    def sent_owner(owner, carry):
        pl.when(owner != seq)(to_owner(owner).wait_send)
        return carry

    lax.fori_loop(0, PBLK, sent_owner, 0)
    pl.when(jnp.logical_not(in_prompt))(to_partner.wait_send)

    def each(copies, what):
        def run():
            for copy in copies:
                getattr(copy, what)()

        return run

    pl.when(section < 3)(each(next_copies, "wait_send"))
    pl.when(section > 0)(each(next_copies, "wait_recv"))
    pl.when(section == 0)(each(zero_next, "wait"))
    pl.when(is_last)(each(zero_prev, "wait"))
    pl.when(section > 0)(each(prev_copies, "wait_send"))
    pl.when(section < 3)(each(prev_copies, "wait_recv"))


def per_device(
    hidden_in,
    saved_hidden,
    grad_in,
    norm_gain,
    w_query,
    w_key,
    w_value,
    w_out,
    head,
    block_table,
    resp_lengths,
    pairs,
):
    seq = lax.axis_index("seq")
    in_prompt = seq < PBLK
    answer = jnp.clip((seq - PBLK) // 2, 0, RESP - 1)
    half = seq % 2
    answers = jnp.arange(RESP, dtype=jnp.int32)
    length = jnp.sum(jnp.where(answers == answer, resp_lengths, 0))
    own_block = jnp.sum(jnp.where(jnp.arange(PBLK, dtype=jnp.int32) == seq, block_table, 0))
    first_pos = jnp.where(in_prompt, own_block * BLK, PROMPT + half * BLK)
    pair_pos = jnp.where(in_prompt, FAR, PROMPT + jnp.arange(2, dtype=jnp.int32) * BLK)
    limit = jnp.where(in_prompt, FAR, PROMPT + length)
    end_row = jnp.where(in_prompt, -1, length - 1 - half * BLK)
    scalars = jnp.concatenate(
        [block_table * BLK, pair_pos, jnp.stack([limit, first_pos, end_row])]
    ).astype(jnp.int32)
    won = jnp.logical_and(pairs[:, 0:1] == answer, pairs[:, 1:2] == answers[None, :])
    lost = jnp.logical_and(pairs[:, 1:2] == answer, pairs[:, 0:1] == answers[None, :])
    sign = jnp.sum(lost.astype(f32) - won.astype(f32), axis=0)
    sign = jnp.broadcast_to(sign[:, None], (RESP, 128))
    frequency = ROPE_BASE ** (-2.0 * jnp.arange(HD // 2, dtype=f32) / HD)
    position = first_pos + jnp.arange(ROWS, dtype=jnp.int32)
    angles = position.astype(f32)[:, None] * frequency[None, :]
    cosine, sine = jnp.cos(angles), jnp.sin(angles)
    cosine = jnp.concatenate([cosine, cosine], axis=1)
    sine = jnp.concatenate([-sine, sine], axis=1)

    any_spec = pl.BlockSpec(memory_space=pl.ANY)
    vmem = pl.BlockSpec(memory_space=pltpu.VMEM)
    dma = pltpu.SemaphoreType.DMA
    out = jax.ShapeDtypeStruct((1, ROWS, D), bf16)
    return pl.pallas_call(
        layer_kernel,
        out_shape=(out, out),
        in_specs=[pl.BlockSpec(memory_space=pltpu.SMEM)] + [any_spec] * 7 + [vmem] * 5,
        out_specs=(any_spec, any_spec),
        scratch_shapes=[
            pltpu.VMEM((ROWS, D), bf16),
            pltpu.VMEM((ROWS, D), bf16),
            pltpu.VMEM((ROWS, D), bf16),
            pltpu.VMEM((64, 2 * ROWS, 128), bf16),
            pltpu.VMEM((SEQ, 256, QKV), bf16),
            pltpu.VMEM((SEQ, 16, D), bf16),
            pltpu.VMEM((2 * ROWS, QKV), f32),
            pltpu.VMEM((2, QH * ROWS, HD), bf16),
            pltpu.VMEM((PBLK + 2, BLK, 512), bf16),
            pltpu.VMEM((2, ROWS, QH * HD), bf16),
            pltpu.VMEM((ROWS, D), bf16),
            pltpu.VMEM((QH * ROWS, HD), bf16),
            pltpu.VMEM((PBLK + 2, BLK, 256), bf16),
            pltpu.VMEM((SEQ, BLK, 256), bf16),
            pltpu.VMEM((8, 128), f32),
            pltpu.VMEM((PBLK, 8, 128), f32),
            pltpu.VMEM((ROWS, QKV), bf16),
            pltpu.VMEM((ROWS, D), bf16),
            pltpu.VMEM((ROWS, OUT_COLS), bf16),
            dma((7,)),
            dma((1,)),
            dma((90,)),
            dma((1,)),
            dma((90,)),
            dma((84,)),
            dma((90,)),
            dma((2,)),
            dma((PBLK + 1,)),
            dma((SEQ,)),
            dma((PBLK,)),
            dma((PBLK,)),
            dma((OUT_STEPS,)),
            dma((OUT_STEPS,)),
            dma((BACK_STEPS,)),
            dma((BACK_STEPS,)),
            dma((OUT_STEPS,)),
        ],
        compiler_params=pltpu.CompilerParams(
            collective_id=0, has_side_effects=True, vmem_limit_bytes=60 * 1024 * 1024
        ),
        cost_estimate=pl.CostEstimate(
            flops=12_000_000_000, bytes_accessed=12_000_000, transcendentals=4_000_000
        ),
    )(
        scalars,
        hidden_in[0],
        saved_hidden[0],
        grad_in[0],
        w_query[0],
        w_key[0],
        w_value[0],
        w_out[0],
        norm_gain,
        head[None, :],
        cosine,
        sine,
        sign,
    )


def solution(mesh):
    rows = P("section", "seq", None)
    return jax.shard_map(
        per_device,
        mesh=mesh,
        in_specs=(rows, rows, rows, P("section", None), rows, rows, rows, rows, P(), P(), P(), P()),
        out_specs=(rows, rows),
        check_vma=False,
    )
```

time: 1070 us -> 229 us (0.21)
  waiting for transfers between devices: 555 us -> 0 us
  Pallas kernels: 0 us -> 215 us
  other arithmetic: 152 us -> 4.55 us
  local copies, waits for them, and re-layouts: 115 us -> 6.63 us
  matrix products: 88.6 us -> 0 us
  blocking collectives: 80.1 us -> 0 us
  starting transfers between devices: 44.9 us -> 0 us
  loops' own time: 18.5 us -> 0 us
  between operations: 14.8 us -> 2.68 us
    all_gather x6 -> x0, waiting for transfers between devices: 382 us -> none  [the longest x1 103 us: per_device(): lax.all_gather(w_query[0], 'seq', axis=0, tiled=True)]
    pallas_call x0 -> x1, Pallas kernels: none -> 215 us  [per_device(): pl.pallas_call(layer_kernel, out_shape=(out, out), in_specs=[pl.BlockSpec...]
    unnamed x8 -> x0, waiting for transfers between devices: 149 us -> none
    dot_general x83 -> x0, matrix products: 88.6 us -> none  [the longest x16 19 us: forward_update(): jnp.einsum('hqk,kd->hqd', weights.astype(jnp.bfloat16), key_block[:, HD:]...]
    psum x1 -> x0, blocking collectives: 80.1 us -> none  [per_device(): rewards = lax.psum(partial_rewards, 'seq')]
    ppermute x2 -> x0, starting transfers between devices: 44.5 us -> none  [from_behind(): return lax.ppermute(value, axis, pairs)]
    select_n x72 -> x1, other arithmetic: 32.5 us -> 0.01 us  [per_device(): jnp.where(in_prompt, FAR, PROMPT + jnp.arange(2, dtype=jnp.int32) * BLK)]
    dynamic_slice x24 -> x0, local copies, waits for them, and re-layouts: 29.9 us -> none  [sweep(): running, _ = lax.scan(advance, running, (stacked, starts))]
  transfers between devices with their start and end apart: 9 -> 0, of which waited for: 8 -> 0; matrix products, arithmetic and copies ran while one was open for 12% -> 0% of each run, Pallas kernels for 0% -> 0%
where the time goes in v1:
time: 229 us
  Pallas kernels  215 us (94%)
  local copies, waits for them, and re-layouts  6.63 us (3%)
  other arithmetic  4.55 us (2%)
  between operations  2.68 us (1%)
    pallas_call x1, Pallas kernels, per_device(): pl.pallas_call(layer_kernel, out_shape=(out, out), in_specs=[pl.BlockSpec...  215 us

profile of v1, /device:TPU:1, one launch (start us, length us, event | category | flops | bytes accessed | tf_op | source)
XLA Modules:
  0.0 229.1 jit_solution(4395225372518159322)
XLA Ops:
  0.7 1.3 fusion.3
  3.3 1.3 fusion.4
  5.3 0.6 concatenate.9.scalars
  5.9 0.8 compare_bitcast_fusion.1
  6.7 0.8 slice_bitcast_fusion
  7.4 0.1 subtract_reduce_fusion
  7.5 0.7 broadcast_in_dim.29.sign
  8.2 0.3 fusion
  8.5 0.8 pad_maximum_fusion
  9.3 215.3 %shard_map.131 = (bf16[1,128,8192]{2,1,0:T(8,128)(2,1)}, bf16[1,128,8192]{2,1,0:T(8,128)(2,1)}) custom-call(s32[21]{0:T(128)} %concatenate.9.scalars, bf16[128,8192]{1,0:T(8,128)(2,1)} %bitcast.19, bf16[128,8192]{1,0:T(8,128)(2,1)} %bitcast.20, bf16[128,8192]{1,0:T(8,128)(2,1)} %bitcast.21, bf16[256,512]{1,0:T(8,128)(2,1)} %bitcast.22, ...), custom_call_target="tpu_custom_call" | custom-call | flops 12000000000 | bytes 12000000 | tf_op jit(solution)/shard_map/pallas_call | solution.py:739
  224.6 0.0 copy-start
  224.6 3.2 %copy.16 = bf16[1,128,8192]{2,1,0:T(8,128)(2,1)} copy(bf16[1,128,8192]{2,1,0:T(8,128)(2,1)} %get-tuple-element.15) | data formatting | bytes 4194304
  227.8 0.0 copy-done
  227.8 1.3 copy.17
  (3 shorter events, 0.0 us)
Async XLA Ops:
  224.6 3.3 %copy-start = (bf16[1,128,8192]{2,1,0:T(8,128)(2,1)S(1)}, bf16[1,128,8192]{2,1,0:T(8,128)(2,1)}, u32[]{:S(2)}) copy-start(bf16[1,128,8192]{2,1,0:T(8,128)(2,1)} %get-tuple-element.16) | copy-start | bytes 6291460

commit v2 on v1

v2 whole, which is shorter than its diff:
```python
import math

import jax
import jax.numpy as jnp
import numpy as np
from jax import lax
from jax.experimental import pallas as pl
from jax.experimental.pallas import tpu as pltpu
from jax.sharding import PartitionSpec as P

HD = 128
QH = 4
RESP = 8
PAIRS = 28
SECTIONS = 4
BLK = 128
D = 8192
ROWS = 128
SEQ = 32
PBLK = 16
PROMPT = 2048
QKV = 768
EPSILON = 1e-05
ROPE_BASE = 500000.0
LOSS_SCALE = 1024.0
NEGATIVE = -1e30
FAR = 1 << 30
SCALE = HD**-0.5
LOG2 = SCALE / math.log(2.0)
OUT_COLS = 1024
OUT_STEPS = D // OUT_COLS
BACK_COLS = 512
BACK_STEPS = D // BACK_COLS

f32 = jnp.float32
bf16 = jnp.bfloat16

FIRST = ((0, 0), (1, 0), (0, 1), (0, 3), (1, 1), (1, 3), (0, 2), (1, 2))
LAST = (0, 1, 3, 2)
STEPS = 10
WAYS = ((True, "xz"), (True, "zx"), (False, "xz"), (False, "zx"))


def nt(a, b):
    return lax.dot_general(a, b, (((1,), (1,)), ((), ())), preferred_element_type=f32)


def tn(a, b):
    return lax.dot_general(a, b, (((0,), (0,)), ((), ())), preferred_element_type=f32)


def nn(a, b):
    return jnp.dot(a, b, preferred_element_type=f32)


class Place:
    def __init__(self):
        self.seq = lax.axis_index("seq")
        z, y, x = self.seq // 8, lax.rem(self.seq // 4, 2), lax.rem(self.seq, 4)
        self.zs = [lax.rem(z + d, 4) for d in range(4)]
        self.ys = [lax.rem(y + d, 2) * 4 for d in range(2)]
        self.xs = [lax.rem(x + d, 4) for d in range(4)]
        self.z_rows = [d * 8 for d in self.zs]

    def at(self, dz=0, dy=0, dx=0):
        return self.z_rows[dz % 4] + self.ys[dy % 2] + self.xs[dx % 4]


class Part:
    def __init__(self, place, view, y_first, axes, send_sem, recv_sems, base):
        self.place, self.view, self.y_first, self.axes = place, view, y_first, axes
        self.send_sem, self.recv_sems = send_sem, recv_sems
        self.slots = {}
        for dy in range(2):
            for da in range(4):
                for db in range(4):
                    if y_first:
                        halves = 2 if (da == 2 and db == 0) or db == 2 else 1
                    else:
                        halves = 2 if dy == 0 and ((da == 2 and db == 0) or db == 2) else 1
                    for sub in range(halves):
                        if (dy, da, db) != (0, 0, 0):
                            self.slots[(dy, da, db, sub)] = base + len(self.slots)

    def origin(self, dy, da, db):
        dx, dz = (da, db) if self.axes == "xz" else (db, da)
        return self.place.at(dz, dy, dx)

    def push(self, dy, da, db, axis, step=1, sub=None):
        if axis == "y":
            target, key = self.place.at(0, 1, 0), (1 - dy, da, db, 0)
        else:
            along_x = (axis == "a") == (self.axes == "xz")
            target = self.place.at(0, 0, step) if along_x else self.place.at(step, 0, 0)
            if axis == "a":
                key = (dy, (da - step) % 4, db, sub or 0)
            else:
                key = (dy, da, (db - step) % 4, sub or 0)
        ref = self.view(self.origin(dy, da, db), sub)
        pltpu.make_async_remote_copy(
            src_ref=ref,
            dst_ref=ref,
            send_sem=self.send_sem.at[0],
            recv_sem=self.recv_sems.at[self.slots[key]],
            device_id={"seq": target},
            device_id_type=pl.DeviceIdType.MESH,
        ).start()

    def take(self, dy, da, db, sub=None):
        ref = self.view(self.origin(dy, da, db), sub)
        pltpu.make_async_remote_copy(
            src_ref=ref,
            dst_ref=ref,
            send_sem=self.send_sem.at[0],
            recv_sem=self.recv_sems.at[self.slots[(dy, da, db, sub or 0)]],
            device_id={"seq": self.place.at(0, 1, 0)},
            device_id_type=pl.DeviceIdType.MESH,
        ).wait_recv()

    def both(self, dy, da, db, axis):
        self.push(dy, da, db, axis, 1)
        self.push(dy, da, db, axis, -1)

    def begin(self):
        self.push(0, 0, 0, "y")
        self.both(0, 0, 0, "a")
        self.both(0, 0, 0, "b")

    def from_first_ring(self, dy, da):
        if da == 2:
            self.take(dy, 2, 0, 0)
            self.take(dy, 2, 0, 1)
        elif (dy, da) != (0, 0):
            self.take(dy, da, 0)
            if da == 0:
                self.both(dy, 0, 0, "a")
            else:
                self.push(dy, da, 0, "a", -1 if da == 1 else 1, 1 if da == 1 else 0)
        if (dy, da) != (0, 0):
            self.both(dy, da, 0, "b")
            if not self.y_first:
                self.push(dy, da, 0, "y")

    def from_second_ring(self, dy, da):
        for db in (1, 3):
            self.take(dy, da, db)
            self.push(dy, da, db, "b", -1 if db == 1 else 1, 1 if db == 1 else 0)
            if not self.y_first:
                self.push(dy, da, db, "y")

    def across_second_ring(self, dy, da):
        self.take(dy, da, 2, 0)
        self.take(dy, da, 2, 1)
        if not self.y_first:
            self.push(dy, da, 2, "y")

    def step(self, k):
        order = FIRST if self.y_first else tuple((0, da) for da in LAST)
        here = []
        if k < len(order):
            self.from_first_ring(*order[k])
        if 1 <= k <= len(order):
            dy, da = order[k - 1]
            self.from_second_ring(dy, da)
            here += [self.origin(dy, da, db) for db in (0, 1, 3)]
        if 2 <= k <= len(order) + 1:
            dy, da = order[k - 2]
            self.across_second_ring(dy, da)
            here.append(self.origin(dy, da, 2))
        if not self.y_first and STEPS - 4 <= k:
            da = LAST[k - (STEPS - 4)]
            for db in (0, 1, 3, 2):
                self.take(1, da, db)
                here.append(self.origin(1, da, db))
        return here


class Gather:
    def __init__(self, place, views, send_sem, recv_sems):
        self.send_sem, self.parts, base = send_sem, [], 0
        for view, (y_first, axes) in zip(views, WAYS):
            part = Part(place, view, y_first, axes, send_sem, recv_sems, base)
            base += len(part.slots)
            self.parts.append(part)
        self.place = place

    def begin(self):
        for part in self.parts:
            part.begin()

    def step(self, k):
        return [(i, o) for i, part in enumerate(self.parts) for o in part.step(k)]

    def finish(self, whole):
        pltpu.make_async_remote_copy(
            src_ref=whole,
            dst_ref=whole,
            send_sem=self.send_sem.at[0],
            recv_sem=self.send_sem.at[0],
            device_id={"seq": self.place.at(0, 1, 0)},
            device_id_type=pl.DeviceIdType.MESH,
        ).wait_send()


def layer_kernel(
    block_table,
    lengths,
    pairs,
    hid_hbm,
    sav_hbm,
    gin_hbm,
    wq_hbm,
    wk_hbm,
    wv_hbm,
    wo_hbm,
    gain,
    head,
    cos_in,
    sin_in,
    cos_block,
    sin_block,
    nh_hbm,
    pg_hbm,
    key_pos_of,
    hid,
    src,
    cot,
    xn,
    wqkv,
    wout,
    acc,
    queries,
    kv,
    pair_kv,
    mixed,
    layer_out,
    squares,
    products,
    mixing,
    dheads,
    dkv,
    pair_dkv,
    landed,
    pair_landed,
    column,
    column_landed,
    tiles,
    back,
    grad,
    zero,
    load_sems,
    weight_send,
    g1_recv,
    g2_recv,
    kvz_send,
    kvz_recv,
    kv_send,
    kv_recv,
    pair_sems,
    rs_send,
    rs_recv,
    pair_back_sems,
    column_send,
    column_recv,
    tile_send,
    tile_recv,
    next_send,
    next_recv,
    prev_send,
    prev_recv,
    zero_sems,
):
    place = Place()
    seq, z = place.seq, place.zs[0]
    own = place.ys[0] + place.xs[0]
    section = lax.axis_index("section")
    is_last = section == SECTIONS - 1
    not_last = section < SECTIONS - 1
    parity = seq % 2
    partner = seq + 1 - 2 * parity
    in_prompt = seq < PBLK
    in_answer = seq >= PBLK

    def other(index):
        return {"seq": index}

    def beside(j):
        return lax.rem(own + j, 8)

    loads = [
        pltpu.make_async_copy(wk_hbm.at[0], wqkv.at[seq, 4], load_sems.at[0]),
        pltpu.make_async_copy(wv_hbm.at[0], wqkv.at[seq, 5], load_sems.at[1]),
    ]
    for h in range(QH):
        loads.append(
            pltpu.make_async_copy(
                wq_hbm.at[0, :, pl.ds(h * HD, HD)], wqkv.at[seq, h], load_sems.at[2 + h]
            )
        )
    hid_load = pltpu.make_async_copy(hid_hbm.at[0], hid, load_sems.at[6])
    saved_load = pltpu.make_async_copy(sav_hbm.at[0], src, load_sems.at[7])
    again_load = pltpu.make_async_copy(hid_hbm.at[0], src, load_sems.at[7])
    wout_load = pltpu.make_async_copy(wo_hbm.at[0], wout.at[seq], load_sems.at[8])
    cot_load = pltpu.make_async_copy(gin_hbm.at[0], cot, load_sems.at[9])
    for load in loads:
        load.start()
    hid_load.start()
    pl.when(not_last)(saved_load.start)
    pl.when(is_last)(again_load.start)
    wout_load.start()
    cot_load.start()

    barrier = pltpu.get_barrier_semaphore()

    def greet(index):
        pl.semaphore_signal(
            barrier, inc=1, device_id=other(index), device_id_type=pl.DeviceIdType.MESH
        )

    for j in range(1, 8):
        greet(z * 8 + beside(j))
    for dz in range(1, 4):
        greet(place.at(dz))
    for step in (1, 3):
        pl.semaphore_signal(
            barrier,
            inc=1,
            device_id={"section": (section + step) % 4},
            device_id_type=pl.DeviceIdType.MESH,
        )

    half = seq % 2
    answer = jnp.maximum(seq - PBLK, 0) // 2
    own_block = jnp.where(in_prompt, block_table[seq % PBLK], PBLK + half)
    length = lengths[answer]
    first_pos = own_block * BLK
    limit = jnp.where(in_prompt, FAR, PROMPT + length)
    end_row = jnp.where(in_prompt, -1, length - 1 - half * BLK)
    for b in range(PBLK):
        key_pos_of[b] = block_table[b] * BLK
    for b in range(2):
        key_pos_of[PBLK + b] = jnp.where(in_prompt, FAR, PROMPT + b * BLK)
    cos_b, sin_b = cos_block[own_block], sin_block[own_block]
    cos = cos_in[...] * cos_b - sin_in[...] * sin_b
    sin = sin_in[...] * cos_b + cos_in[...] * sin_b

    for load in loads:
        load.wait()
    pl.semaphore_wait(barrier, 12)

    def qkv_view(first, count):
        def view(o, sub):
            if sub is None:
                return wqkv.at[o, pl.ds(first, count)]
            if count == 2:
                return wqkv.at[o, pl.ds(first + sub, 1)]
            return wqkv.at[o, pl.ds(first, 1), pl.ds(sub * 128, 128), :]

        return view

    def out_view(first, size):
        def view(o, sub):
            if sub is None:
                return wout.at[o, :, pl.ds(first, size)]
            return wout.at[o, :, pl.ds(first + sub * (size // 2), size // 2)]

        return view

    groups = ((0, 2), (2, 2), (4, 1), (5, 1))
    g1 = Gather(place, [qkv_view(*g) for g in groups], weight_send.at[pl.ds(0, 1)], g1_recv)
    columns = ((0, 2816), (2816, 2816), (5632, 1280), (6912, 1280))
    g2 = Gather(place, [out_view(*c) for c in columns], weight_send.at[pl.ds(1, 1)], g2_recv)
    g1.begin()

    acc[...] = jnp.zeros_like(acc)
    zero[...] = jnp.zeros_like(zero)

    def inverse_rms(buf):
        def body(i, total):
            wide = buf[:, pl.ds(pl.multiple_of(i * 512, 512), 512)].astype(f32)
            wide = wide * wide
            return total + (
                (wide[:, :128] + wide[:, 128:256]) + (wide[:, 256:384] + wide[:, 384:])
            )

        total = lax.fori_loop(0, 16, body, jnp.zeros((ROWS, 128), f32))
        return lax.rsqrt(jnp.sum(total, axis=1, keepdims=True) * (1.0 / D) + EPSILON)

    def normalize(buf, row):
        inv = inverse_rms(buf)

        def body(i, carry):
            at = pl.ds(pl.multiple_of(i * 256, 256), 256)
            xn[i, pl.ds(row, ROWS), :] = (buf[:, at].astype(f32) * inv * gain[:, at]).astype(bf16)
            return carry

        lax.fori_loop(0, SEQ, body, 0)
        return inv

    def project(here):
        for i, o in here:
            first, count = groups[i]
            w = jnp.concatenate([wqkv[o, g] for g in range(first, first + count)], axis=1)
            acc[:, first * HD : (first + count) * HD] += nn(xn[o], w)

    hid_load.wait()
    normalize(hid, 0)
    first_here = g1.step(0)
    saved_load.wait()
    inv_src = normalize(src, ROWS)
    wout_load.wait()
    cot_load.wait()
    first_here += g1.step(1)
    project(first_here)
    for k in range(2, STEPS):
        if k == 5:
            g2.begin()
        project(g1.step(k))
        if k >= 7:
            g2.step(k - 7)

    def rotated(t, g):
        u = acc[t * ROWS : (t + 1) * ROWS, g * HD : (g + 1) * HD]
        return (u * cos + pltpu.roll(u, HD // 2, 1) * sin).astype(bf16)

    for t in range(2):
        pair_kv[parity, :, t * 256 : t * 256 + 128] = rotated(t, 4)
        pair_kv[parity, :, t * 256 + 128 : t * 256 + 256] = acc[
            t * ROWS : (t + 1) * ROWS, 640:768
        ].astype(bf16)

    pair_copy = pltpu.make_async_remote_copy(
        src_ref=pair_kv.at[parity],
        dst_ref=pair_kv.at[parity],
        send_sem=pair_sems.at[0],
        recv_sem=pair_sems.at[1],
        device_id=other(partner),
        device_id_type=pl.DeviceIdType.MESH,
    )

    def along_z(dz):
        return pltpu.make_async_remote_copy(
            src_ref=kv.at[z % 2, own],
            dst_ref=kv.at[z % 2, own],
            send_sem=kvz_send.at[dz],
            recv_sem=kvz_recv.at[z % 2],
            device_id=other(place.at(dz)),
            device_id_type=pl.DeviceIdType.MESH,
        )

    def send_along_z():
        kv[z, own] = pair_kv[parity]
        for dz in (1, 3, 2):
            along_z(dz).start()

    pl.when(in_prompt)(send_along_z)
    pair_copy.start()

    kv_sent, kv_slots = [], {}

    def kv_piece(dy, dx, rows):
        return kv.at[:, place.ys[dy % 2] + place.xs[dx % 4], pl.ds(*rows)]

    def kv_slot(dy, dx, rows):
        return kv_slots.setdefault((dy % 2, dx % 4, rows), len(kv_slots))

    def kv_push(dy, dx, rows, to_y, to_x):
        ref = kv_piece(dy, dx, rows)
        copy = pltpu.make_async_remote_copy(
            src_ref=ref,
            dst_ref=ref,
            send_sem=kv_send.at[len(kv_sent)],
            recv_sem=kv_recv.at[kv_slot(dy - to_y, dx - to_x, rows)],
            device_id=other(place.at(0, to_y, to_x)),
            device_id_type=pl.DeviceIdType.MESH,
        )
        kv_sent.append(copy)
        copy.start()

    def kv_take(dy, dx, rows):
        ref = kv_piece(dy, dx, rows)
        pltpu.make_async_remote_copy(
            src_ref=ref,
            dst_ref=ref,
            send_sem=kv_send.at[0],
            recv_sem=kv_recv.at[kv_slot(dy, dx, rows)],
            device_id=other(place.at(0, 1, 0)),
            device_id_type=pl.DeviceIdType.MESH,
        ).wait_recv()

    y_rows, x_rows = (0, 64), (64, 64)

    def halves_of(rows):
        return (rows[0], 32), (rows[0] + 32, 32)

    def kv_ring(dy, rows):
        kv_push(dy, 0, rows, 0, 1)
        kv_push(dy, 0, rows, 0, -1)

    def kv_ring_on(dy, rows):
        low, high = halves_of(rows)
        kv_take(dy, 1, rows)
        kv_push(dy, 1, high, 0, -1)
        kv_take(dy, 3, rows)
        kv_push(dy, 3, low, 0, 1)

    def kv_ring_end(dy, rows):
        for part in halves_of(rows):
            kv_take(dy, 2, part)

    def kv_step(k):
        if k == 0:
            for source in range(2):

                def wait(source=source):
                    pltpu.make_async_remote_copy(
                        src_ref=kv.at[source, own],
                        dst_ref=kv.at[source, own],
                        send_sem=kvz_send.at[0],
                        recv_sem=kvz_recv.at[source],
                        device_id=other(partner),
                        device_id_type=pl.DeviceIdType.MESH,
                    ).wait_recv()

                pl.when(z != source)(wait)
            kv_push(0, 0, y_rows, 1, 0)
            kv_ring(0, x_rows)
            kv_ring(0, y_rows)
            kv_push(0, 0, x_rows, 1, 0)
        elif k == 1:
            kv_take(1, 0, y_rows)
            kv_ring(1, y_rows)
            kv_ring_on(0, x_rows)
            kv_push(0, 1, x_rows, 1, 0)
            kv_push(0, 3, x_rows, 1, 0)
            kv_ring_on(0, y_rows)
        elif k == 2:
            kv_ring_end(0, x_rows)
            kv_push(0, 2, x_rows, 1, 0)
            kv_ring_on(1, y_rows)
        else:
            kv_ring_end(0, y_rows)
            kv_ring_end(1, y_rows)
            for dx in range(4):
                kv_take(1, dx, x_rows)

    g2.step(3)
    kv_step(0)
    for t in range(2):
        for h in range(QH):
            queries[t, h * HD : (h + 1) * HD, :] = rotated(t, h)
    for k in range(1, 4):
        g2.step(3 + k)
        kv_step(k)
    pair_copy.wait_send()
    pltpu.make_async_remote_copy(
        src_ref=pair_kv.at[parity],
        dst_ref=pair_kv.at[1 - parity],
        send_sem=pair_sems.at[0],
        recv_sem=pair_sems.at[1],
        device_id=other(partner),
        device_id_type=pl.DeviceIdType.MESH,
    ).wait_recv()

    across = lax.broadcasted_iota(jnp.int32, (1, QH * ROWS), 1) % ROWS
    query_pos = first_pos + across
    down = lax.broadcasted_iota(jnp.int32, (2 * BLK, 1), 0)

    def allowed(c):
        key_pos = jnp.where(
            down < BLK, key_pos_of[2 * c] + down, key_pos_of[2 * c + 1] + (down - BLK)
        )
        key_pos = jnp.where(key_pos < limit, key_pos, FAR)
        return key_pos <= query_pos

    def block_of(c, at):
        if isinstance(c, int) and c == PBLK // 2:
            return pair_kv[:, :, at].reshape(2 * BLK, HD)
        side, first = c // 4, lax.rem(c, 4) * 2
        return kv[pl.ds(side, 1), pl.ds(first, 2), :, at].reshape(2 * BLK, HD)

    def keys_of(c, t):
        return block_of(c, slice(t * 256, t * 256 + 128))

    def values_of(c, t):
        return block_of(c, slice(t * 256 + 128, t * 256 + 256))

    def attend(t, between):
        q = queries[t]

        def chunk(c, carry):
            row_max, total, weighted = carry
            scores = jnp.where(allowed(c), nt(keys_of(c, t), q), NEGATIVE)
            new_max = jnp.maximum(row_max, jnp.max(scores, axis=0, keepdims=True))
            weights = jnp.exp2((scores - new_max) * LOG2)
            factor = jnp.exp2((row_max - new_max) * LOG2)
            total = total * factor + jnp.sum(weights, axis=0, keepdims=True)
            weighted = weighted * factor + tn(values_of(c, t), weights.astype(bf16))
            return new_max, total, weighted

        carry = (
            jnp.full((1, QH * ROWS), NEGATIVE, f32),
            jnp.zeros((1, QH * ROWS), f32),
            jnp.zeros((HD, QH * ROWS), f32),
        )
        for start, then in zip((0, 4), between):
            carry = lax.fori_loop(start, start + 4, chunk, carry)
            for k in then:
                g2.step(k)
        carry = chunk(PBLK // 2, carry)
        row_max, total, weighted = carry
        weighted = weighted / total
        for h in range(QH):
            mixed[t, :, h * HD : (h + 1) * HD] = weighted[:, h * HD : (h + 1) * HD].T.astype(bf16)
        return row_max * LOG2 + jnp.log2(total)

    log_total = attend(1, ((7,), (8,)))
    attend(0, ((9,), ()))

    next_copies = [
        pltpu.make_async_remote_copy(
            src_ref=layer_out.at[:, pl.ds(c * OUT_COLS, OUT_COLS)],
            dst_ref=nh_hbm.at[0, :, pl.ds(c * OUT_COLS, OUT_COLS)],
            send_sem=next_send.at[c],
            recv_sem=next_recv.at[c],
            device_id={"section": (section + 1) % 4},
            device_id_type=pl.DeviceIdType.MESH,
        )
        for c in range(OUT_STEPS)
    ]

    def output(steps):
        mixed_now = mixed[0]
        for c in steps:
            at = pl.ds(c * OUT_COLS, OUT_COLS)
            w = wout[:, :, at].reshape(QH * HD, OUT_COLS)
            y = (nn(mixed_now, w) + hid[:, at].astype(f32)).astype(bf16)
            layer_out[:, at] = y
            pl.when(not_last)(next_copies[c].start)

    def measure_output():
        def body(i, carry):
            square, product = carry
            wide = layer_out[:, pl.ds(pl.multiple_of(i * 128, 128), 128)].astype(f32)
            return square + wide * wide, product + wide * head[pl.ds(i, 1), :]

        none = jnp.zeros((ROWS, 128), f32)
        squares[...], products[...] = lax.fori_loop(0, D // 128, body, (none, none))

    def mix_back(steps):
        def body(c, total):
            at = pl.ds(pl.multiple_of(c * OUT_COLS, OUT_COLS), OUT_COLS)
            return total + nt(cot[:, at], wout[:, :, at].reshape(QH * HD, OUT_COLS))

        mixing[...] = lax.fori_loop(steps[0], steps[1], body, mixing[...])

    mixing[...] = jnp.zeros_like(mixing)
    pl.when(not_last)(lambda: mix_back((0, OUT_STEPS)))

    zero_next = [
        pltpu.make_async_copy(
            zero, nh_hbm.at[0, :, pl.ds(c * OUT_COLS, OUT_COLS)], zero_sems.at[c]
        )
        for c in range(OUT_STEPS)
    ]
    zero_prev = [
        pltpu.make_async_copy(
            zero, pg_hbm.at[0, :, pl.ds(c * OUT_COLS, OUT_COLS)], zero_sems.at[c]
        )
        for c in range(OUT_STEPS)
    ]

    def each(copies, what):
        def run():
            for copy in copies:
                getattr(copy, what)()

        return run

    pl.when(section == 0)(each(zero_next, "start"))
    pl.when(is_last)(each(zero_prev, "start"))

    def reward_rows():
        output(range(OUT_STEPS))
        measure_output()
        mean_square = jnp.sum(squares[...], axis=1, keepdims=True) * (1.0 / D)
        dots = jnp.sum(products[...], axis=1, keepdims=True)
        inv = lax.rsqrt(mean_square + EPSILON)
        rows = lax.broadcasted_iota(jnp.int32, (ROWS, 1), 0)
        hit = rows == end_row
        reward = jnp.sum(jnp.where(hit, dots * inv, 0.0), axis=0, keepdims=True)
        side = z - 2
        tiles[side, own] = jnp.broadcast_to(reward, (8, 128))
        to_z = pltpu.make_async_remote_copy(
            src_ref=tiles.at[side, own],
            dst_ref=tiles.at[side, own],
            send_sem=tile_send.at[0],
            recv_sem=tile_recv.at[8],
            device_id=other((3 - side) * 8 + own),
            device_id_type=pl.DeviceIdType.MESH,
        )
        to_z.start()
        down8 = lax.broadcasted_iota(jnp.int32, (RESP, 128), 0)
        sign = jnp.zeros((RESP, 128), f32)
        for p in range(PAIRS):
            won, lost = pairs[p, 0], pairs[p, 1]
            sign += jnp.where(lost == answer, (down8 == won).astype(f32), 0.0)
            sign -= jnp.where(won == answer, (down8 == lost).astype(f32), 0.0)
        pltpu.make_async_remote_copy(
            src_ref=tiles.at[1 - side, own],
            dst_ref=tiles.at[1 - side, own],
            send_sem=tile_send.at[0],
            recv_sem=tile_recv.at[8],
            device_id=other(partner),
            device_id_type=pl.DeviceIdType.MESH,
        ).wait_recv()
        copies = [to_z]
        for j in range(1, 8):
            copies.append(
                pltpu.make_async_remote_copy(
                    src_ref=tiles.at[:, own],
                    dst_ref=tiles.at[:, own],
                    send_sem=tile_send.at[j],
                    recv_sem=tile_recv.at[own],
                    device_id=other(z * 8 + beside(j)),
                    device_id_type=pl.DeviceIdType.MESH,
                )
            )
            copies[-1].start()
        for j in range(1, 8):
            pltpu.make_async_remote_copy(
                src_ref=tiles.at[:, own],
                dst_ref=tiles.at[:, beside(j)],
                send_sem=tile_send.at[0],
                recv_sem=tile_recv.at[beside(j)],
                device_id=other(partner),
                device_id_type=pl.DeviceIdType.MESH,
            ).wait_recv()
        for copy in copies:
            copy.wait_send()
        mine = (tiles[side, own] + tiles[side, own + 1 - 2 * parity])[0:1]
        pull = jnp.zeros((1, 128), f32)
        for r in range(RESP):
            way = sign[r : r + 1, :]
            first = 2 * (r % 4)
            reward_r = (tiles[r // 4, first] + tiles[r // 4, first + 1])[0:1]
            pull += way / (1.0 + jnp.exp(way * (reward_r - mine)))
        pull = pull * (LOSS_SCALE / PAIRS)
        row_grad = jnp.where(hit, jnp.sum(pull, axis=1, keepdims=True) * (1.0 / 128.0), 0.0)
        by_head = row_grad * inv
        by_out = row_grad * (inv * inv * inv) * (dots * (1.0 / D))

        def body(i, carry):
            at = pl.ds(pl.multiple_of(i * 128, 128), 128)
            wide = layer_out[:, at].astype(f32)
            cot[:, at] = (by_head * head[pl.ds(i, 1), :] - wide * by_out).astype(bf16)
            return carry

        lax.fori_loop(0, D // 128, body, 0)
        mix_back((0, OUT_STEPS))

    def no_rewards():
        cot[...] = jnp.zeros_like(cot)

    pl.when(jnp.logical_and(is_last, in_answer))(reward_rows)
    pl.when(jnp.logical_and(is_last, in_prompt))(no_rewards)

    d_mixed = mixing[...].astype(bf16)
    dots = d_mixed.astype(f32) * mixed[1].astype(f32)
    row_dots = []
    for h in range(QH):
        dheads[h * HD : (h + 1) * HD, :] = d_mixed[:, h * HD : (h + 1) * HD]
        row_dots.append(jnp.sum(dots[:, h * HD : (h + 1) * HD].T, axis=0, keepdims=True))
    row_dots = jnp.concatenate(row_dots, axis=1)

    q = queries[1]
    dh = dheads[...]

    def attend_back(c, d_query):
        keys, values = keys_of(c, 1), values_of(c, 1)
        probs = jnp.exp2(jnp.where(allowed(c), nt(keys, q) * LOG2 - log_total, NEGATIVE))
        d_scores = (probs * (nt(values, dh) - row_dots)).astype(bf16)
        d_key = (nn(d_scores, q) * SCALE).astype(bf16)
        d_value = nn(probs.astype(bf16), dh).astype(bf16)
        both = jnp.concatenate([d_key, d_value], axis=1)
        if isinstance(c, int):
            pair_dkv[...] = both.reshape(2, BLK, 2 * HD)
        else:
            dkv[pl.ds(c // 4, 1), pl.ds(lax.rem(c, 4) * 2, 2)] = both.reshape(1, 2, BLK, 2 * HD)
        return d_query + tn(keys, d_scores)

    def to_summer(side, there):
        return pltpu.make_async_remote_copy(
            src_ref=dkv.at[side, there],
            dst_ref=landed.at[own, side],
            send_sem=rs_send.at[side * 8 + there],
            recv_sem=rs_recv.at[own * 2 + side],
            device_id=other(z * 8 + there),
            device_id_type=pl.DeviceIdType.MESH,
        )

    def back_chunk(i, d_query):
        side, pair = i // 4, lax.rem(own // 2 + 1 + i, 4)
        d_query = attend_back(side * 4 + pair, d_query)
        for j in range(2):
            there = pair * 2 + j
            pl.when(there != own)(to_summer(side, there).start)
        return d_query

    d_query = lax.fori_loop(0, 8, back_chunk, jnp.zeros((HD, QH * ROWS), f32))
    d_query = attend_back(PBLK // 2, d_query) * SCALE
    to_partner = pltpu.make_async_remote_copy(
        src_ref=pair_dkv.at[1 - parity],
        dst_ref=pair_landed,
        send_sem=pair_back_sems.at[0],
        recv_sem=pair_back_sems.at[1],
        device_id=other(partner),
        device_id_type=pl.DeviceIdType.MESH,
    )
    pl.when(in_answer)(to_partner.start)

    for h in range(QH):
        u = d_query[:, h * HD : (h + 1) * HD].T
        back[:, h * HD : (h + 1) * HD] = (u * cos - pltpu.roll(u, HD // 2, 1) * sin).astype(bf16)

    pl.when(not_last)(lambda: output(range(OUT_STEPS)))

    def column_copy(side):
        return pltpu.make_async_remote_copy(
            src_ref=column.at[side],
            dst_ref=column_landed.at[z],
            send_sem=column_send.at[side],
            recv_sem=column_recv.at[z],
            device_id=other(side * 8 + own),
            device_id_type=pl.DeviceIdType.MESH,
        )

    for side in range(2):

        def add(j, total, side=side):
            there = beside(j)
            pltpu.make_async_remote_copy(
                src_ref=dkv.at[side, there],
                dst_ref=landed.at[there, side],
                send_sem=rs_send.at[0],
                recv_sem=rs_recv.at[there * 2 + side],
                device_id=other(partner),
                device_id_type=pl.DeviceIdType.MESH,
            ).wait_recv()
            return total + landed[there, side].astype(f32)

        column[side] = lax.fori_loop(1, 8, add, dkv[side, own].astype(f32)).astype(bf16)
        pl.when(z != side)(column_copy(side).start)

    def keep(total):
        u = total[:, :HD]
        back[:, 512:640] = (u * cos - pltpu.roll(u, HD // 2, 1) * sin).astype(bf16)
        back[:, 640:768] = total[:, HD:].astype(bf16)

    def sum_prompt():
        def add(j, total):
            there = lax.rem(z + j, 4)
            pltpu.make_async_remote_copy(
                src_ref=column.at[0],
                dst_ref=column_landed.at[there],
                send_sem=column_send.at[0],
                recv_sem=column_recv.at[there],
                device_id=other(partner),
                device_id_type=pl.DeviceIdType.MESH,
            ).wait_recv()
            return total + column_landed[there].astype(f32)

        keep(lax.fori_loop(1, 4, add, column[z].astype(f32)))

    def sum_answer():
        to_partner.wait_recv()
        keep(pair_dkv[parity].astype(f32) + pair_landed[...].astype(f32))

    pl.when(in_prompt)(sum_prompt)
    pl.when(in_answer)(sum_answer)

    back_all = back[...]
    along = jnp.sum(back_all.astype(f32) * acc[ROWS:, :], axis=1, keepdims=True)
    along = along * (inv_src * inv_src) * (1.0 / D)
    prev_copies = []
    for c in range(BACK_STEPS):
        at = pl.ds(c * BACK_COLS, BACK_COLS)
        w = jnp.concatenate(
            [wqkv[2 * c : 2 * c + 2, g].reshape(BACK_COLS, HD) for g in range(QKV // HD)], axis=1
        )
        u = nt(back_all, w) * gain[:, at]
        grad[:, at] = (
            cot[:, at].astype(f32) + inv_src * u - src[:, at].astype(f32) * along
        ).astype(bf16)
        prev_copies.append(
            pltpu.make_async_remote_copy(
                src_ref=grad.at[:, at],
                dst_ref=pg_hbm.at[0, :, at],
                send_sem=prev_send.at[c],
                recv_sem=prev_recv.at[c],
                device_id={"section": (section + 3) % 4},
                device_id_type=pl.DeviceIdType.MESH,
            )
        )
        pl.when(section > 0)(prev_copies[-1].start)

    g1.finish(wqkv.at[pl.ds(0, SEQ - 1)])
    g2.finish(wout.at[pl.ds(0, SEQ - 1)])
    pl.when(in_prompt)(each([along_z(dz) for dz in (1, 3, 2)], "wait_send"))
    for copy in kv_sent:
        copy.wait_send()
    for side in range(2):

        def sent_on(there, carry, side=side):
            pl.when(there != own)(to_summer(side, there).wait_send)
            return carry

        lax.fori_loop(0, 8, sent_on, 0)
        pl.when(z != side)(column_copy(side).wait_send)
    pl.when(in_answer)(to_partner.wait_send)
    pl.when(not_last)(each(next_copies, "wait_send"))
    pl.when(section > 0)(each(next_copies, "wait_recv"))
    pl.when(section == 0)(each(zero_next, "wait"))
    pl.when(is_last)(each(zero_prev, "wait"))
    pl.when(section > 0)(each(prev_copies, "wait_send"))
    pl.when(not_last)(each(prev_copies, "wait_recv"))


def angle_tables():
    frequency = ROPE_BASE ** (-2.0 * np.arange(HD // 2) / HD)

    def table(positions):
        angles = np.asarray(positions, np.float64)[:, None] * frequency[None, :]
        cosine, sine = np.cos(angles), np.sin(angles)
        return (
            np.concatenate([cosine, cosine], axis=1).astype(np.float32),
            np.concatenate([-sine, sine], axis=1).astype(np.float32),
        )

    within = table(np.arange(BLK))
    blocks = [part[:, None, :] for part in table(np.arange(PBLK + 2) * BLK)]
    return (*within, *blocks)


def per_device(
    hidden_in,
    saved_hidden,
    grad_in,
    norm_gain,
    w_query,
    w_key,
    w_value,
    w_out,
    head,
    block_table,
    resp_lengths,
    pairs,
):
    any_spec = pl.BlockSpec(memory_space=pl.ANY)
    vmem = pl.BlockSpec(memory_space=pltpu.VMEM)
    smem = pl.BlockSpec(memory_space=pltpu.SMEM)
    dma = pltpu.SemaphoreType.DMA
    out = jax.ShapeDtypeStruct((1, ROWS, D), bf16)
    return pl.pallas_call(
        layer_kernel,
        out_shape=(out, out),
        in_specs=[smem] * 3 + [any_spec] * 7 + [vmem] * 6,
        out_specs=(any_spec, any_spec),
        scratch_shapes=[
            pltpu.SMEM((PBLK + 2,), jnp.int32),
            pltpu.VMEM((ROWS, D), bf16),
            pltpu.VMEM((ROWS, D), bf16),
            pltpu.VMEM((ROWS, D), bf16),
            pltpu.VMEM((SEQ, 2 * ROWS, 256), bf16),
            pltpu.VMEM((SEQ, QKV // HD, 256, HD), bf16),
            pltpu.VMEM((SEQ, 16, D), bf16),
            pltpu.VMEM((2 * ROWS, QKV), f32),
            pltpu.VMEM((2, QH * ROWS, HD), bf16),
            pltpu.VMEM((2, 8, BLK, 512), bf16),
            pltpu.VMEM((2, BLK, 512), bf16),
            pltpu.VMEM((2, ROWS, QH * HD), bf16),
            pltpu.VMEM((ROWS, D), bf16),
            pltpu.VMEM((ROWS, 128), f32),
            pltpu.VMEM((ROWS, 128), f32),
            pltpu.VMEM((ROWS, QH * HD), f32),
            pltpu.VMEM((QH * ROWS, HD), bf16),
            pltpu.VMEM((2, 8, BLK, 256), bf16),
            pltpu.VMEM((2, BLK, 256), bf16),
            pltpu.VMEM((8, 2, BLK, 256), bf16),
            pltpu.VMEM((BLK, 256), bf16),
            pltpu.VMEM((2, BLK, 256), bf16),
            pltpu.VMEM((4, BLK, 256), bf16),
            pltpu.VMEM((2, 8, 8, 128), f32),
            pltpu.VMEM((ROWS, QKV), bf16),
            pltpu.VMEM((ROWS, D), bf16),
            pltpu.VMEM((ROWS, OUT_COLS), bf16),
            dma((10,)),
            dma((2,)),
            dma((160,)),
            dma((160,)),
            dma((4,)),
            dma((2,)),
            dma((32,)),
            dma((32,)),
            dma((2,)),
            dma((16,)),
            dma((16,)),
            dma((2,)),
            dma((2,)),
            dma((4,)),
            dma((8,)),
            dma((9,)),
            dma((OUT_STEPS,)),
            dma((OUT_STEPS,)),
            dma((BACK_STEPS,)),
            dma((BACK_STEPS,)),
            dma((OUT_STEPS,)),
        ],
        compiler_params=pltpu.CompilerParams(
            collective_id=0, has_side_effects=True, vmem_limit_bytes=60 * 1024 * 1024
        ),
        cost_estimate=pl.CostEstimate(
            flops=12_000_000_000, bytes_accessed=12_000_000, transcendentals=4_000_000
        ),
    )(
        block_table,
        resp_lengths,
        pairs,
        hidden_in,
        saved_hidden,
        grad_in,
        w_query,
        w_key,
        w_value,
        w_out,
        norm_gain,
        head.reshape(D // 128, 128),
        *angle_tables(),
    )


def solution(mesh):
    rows = P("section", "seq", None)
    return jax.shard_map(
        per_device,
        mesh=mesh,
        in_specs=(rows, rows, rows, P("section", None), rows, rows, rows, rows, P(), P(), P(), P()),
        out_specs=(rows, rows),
        check_vma=False,
    )
```

time: 229 us -> 181 us (0.79)
  Pallas kernels: 215 us -> 173 us
  other arithmetic: 4.55 us -> 0 us
    pallas_call x1, Pallas kernels: 215 us -> 173 us  [per_device(): pl.pallas_call(layer_kernel, out_shape=(out, out), in_specs=[smem] * 3 +...]
    reduce_sum x3 -> x0, other arithmetic: 2.71 us -> none  [the longest x1 1.3 us: per_device(): jnp.sum(jnp.where(jnp.arange(PBLK, dtype=jnp.int32) == seq, block_table, 0))]
    unnamed x4 -> x5, local copies, waits for them, and re-layouts: 4.57 us -> 5.94 us
where the time goes in v2:
time: 181 us; the launch traced here: 180 us
  Pallas kernels  173 us (96%)
  local copies, waits for them, and re-layouts  5.94 us (3%)
    pallas_call x1, Pallas kernels, per_device(): pl.pallas_call(layer_kernel, out_shape=(out, out), in_specs=[smem] * 3 +...  173 us
    unnamed x5, local copies, waits for them, and re-layouts  5.94 us

profile of v2, /device:TPU:1, one launch (start us, length us, event | category | flops | bytes accessed | tf_op | source)
XLA Modules:
  0.0 180.0 jit_solution(17742932023777049855)
XLA Ops:
  0.6 1.4 copy.18.pairs
  2.0 173.4 %shard_map.167 = (bf16[1,128,8192]{2,1,0:T(8,128)(2,1)}, bf16[1,128,8192]{2,1,0:T(8,128)(2,1)}) custom-call(s32[16]{0:T(128)} %block_table.1, s32[8]{0:T(128)} %lengths.1, s32[28,2]{1,0:T(8,128)} %copy.18.pairs, bf16[1,128,8192]{2,1,0:T(8,128)(2,1)} %hid_hbm.1, bf16[1,128,8192]{2,1,0:T(8,128)(2,1)} %sav_hbm.1, bf16[1,128,8192]{2,1,0:T(8,128)(2,1)} %gin_hbm.1, ...), custom_call_target="tpu_custom_call" | custom-call | flops 12000000000 | bytes 12000000 | tf_op jit(solution)/shard_map/pallas_call | solution.py:964
  175.4 0.0 copy-start
  175.5 3.2 %copy.21 = bf16[1,128,8192]{2,1,0:T(8,128)(2,1)} copy(bf16[1,128,8192]{2,1,0:T(8,128)(2,1)} %get-tuple-element.4) | data formatting | bytes 4194304
  178.7 0.0 copy-done
  178.7 1.3 copy.22
Async XLA Ops:
  175.4 3.3 %copy-start = (bf16[1,128,8192]{2,1,0:T(8,128)(2,1)S(1)}, bf16[1,128,8192]{2,1,0:T(8,128)(2,1)}, u32[]{:S(2)}) copy-start(bf16[1,128,8192]{2,1,0:T(8,128)(2,1)} %get-tuple-element.5) | copy-start | bytes 6291460

commit v3 on v2

--- a/solution.py
+++ b/solution.py
@@ -29,16 +29,29 @@
 LOG2 = SCALE / math.log(2.0)
 OUT_COLS = 1024
 OUT_STEPS = D // OUT_COLS
+MIX_COLS = 512
+MIX_STEPS = D // MIX_COLS
+MIX_FIRST = 2 * 2816 // MIX_COLS
 BACK_COLS = 512
 BACK_STEPS = D // BACK_COLS
+ROUND = (2, 7, 12)
 
 f32 = jnp.float32
 bf16 = jnp.bfloat16
 
 FIRST = ((0, 0), (1, 0), (0, 1), (0, 3), (1, 1), (1, 3), (0, 2), (1, 2))
 LAST = (0, 1, 3, 2)
-STEPS = 10
-WAYS = ((True, "xz"), (True, "zx"), (False, "xz"), (False, "zx"))
+LAG_ON, LAG_ACROSS = 2, 4
+STEPS = len(FIRST) + LAG_ACROSS
+QKV_WAYS = (
+    (True, "xz"),
+    (True, "zx"),
+    (True, "xz"),
+    (True, "zx"),
+    (False, "xz"),
+    (False, "zx"),
+)
+OUT_WAYS = ((True, "xz"), (True, "zx"), (False, "xz"), (False, "zx"))
 
 
 def nt(a, b):
@@ -159,12 +172,12 @@
         here = []
         if k < len(order):
             self.from_first_ring(*order[k])
-        if 1 <= k <= len(order):
-            dy, da = order[k - 1]
+        if 0 <= k - LAG_ON < len(order):
+            dy, da = order[k - LAG_ON]
             self.from_second_ring(dy, da)
             here += [self.origin(dy, da, db) for db in (0, 1, 3)]
-        if 2 <= k <= len(order) + 1:
-            dy, da = order[k - 2]
+        if 0 <= k - LAG_ACROSS < len(order):
+            dy, da = order[k - LAG_ACROSS]
             self.across_second_ring(dy, da)
             here.append(self.origin(dy, da, 2))
         if not self.y_first and STEPS - 4 <= k:
@@ -176,9 +189,9 @@
 
 
 class Gather:
-    def __init__(self, place, views, send_sem, recv_sems):
+    def __init__(self, place, views, ways, send_sem, recv_sems):
         self.send_sem, self.parts, base = send_sem, [], 0
-        for view, (y_first, axes) in zip(views, WAYS):
+        for view, (y_first, axes) in zip(views, ways):
             part = Part(place, view, y_first, axes, send_sem, recv_sems, base)
             base += len(part.slots)
             self.parts.append(part)
@@ -188,8 +201,10 @@
         for part in self.parts:
             part.begin()
 
-    def step(self, k):
-        return [(i, o) for i, part in enumerate(self.parts) for o in part.step(k)]
+    def step(self, *steps):
+        if len(steps) == 1 and isinstance(steps[0], int):
+            steps = [(i, steps[0]) for i in range(len(self.parts))]
+        return [(i, o) for i, k in steps if 0 <= k < STEPS for o in self.parts[i].step(k)]
 
     def finish(self, whole):
         pltpu.make_async_remote_copy(
@@ -247,6 +262,7 @@
     tiles,
     back,
     grad,
+    relay,
     zero,
     load_sems,
     weight_send,
@@ -268,6 +284,8 @@
     next_recv,
     prev_send,
     prev_recv,
+    relay_send,
+    relay_recv,
     zero_sems,
 ):
     place = Place()
@@ -280,6 +298,11 @@
     partner = seq + 1 - 2 * parity
     in_prompt = seq < PBLK
     in_answer = seq >= PBLK
+    has_back = section > 0
+    from_grad = jnp.logical_and(has_back, not_last)
+    sends_keys = jnp.logical_and(has_back, jnp.logical_or(not_last, in_answer))
+    last_prompt = jnp.logical_and(is_last, in_prompt)
+    across_y = place.at(0, 1, 0)
 
     def other(index):
         return {"seq": index}
@@ -344,17 +367,21 @@
     cos = cos_in[...] * cos_b - sin_in[...] * sin_b
     sin = sin_in[...] * cos_b + cos_in[...] * sin_b
 
+    pl.semaphore_signal(
+        barrier,
+        inc=1,
+        device_id={"section": (section + 2) % 4, "seq": across_y},
+        device_id_type=pl.DeviceIdType.MESH,
+    )
     for load in loads:
         load.wait()
-    pl.semaphore_wait(barrier, 12)
-
-    def qkv_view(first, count):
+    pl.semaphore_wait(barrier, 13)
+
+    def qkv_view(group):
         def view(o, sub):
             if sub is None:
-                return wqkv.at[o, pl.ds(first, count)]
-            if count == 2:
-                return wqkv.at[o, pl.ds(first + sub, 1)]
-            return wqkv.at[o, pl.ds(first, 1), pl.ds(sub * 128, 128), :]
+                return wqkv.at[o, group]
+            return wqkv.at[o, group, pl.ds(sub * 128, 128), :]
 
         return view
 
@@ -366,10 +393,14 @@
 
         return view
 
-    groups = ((0, 2), (2, 2), (4, 1), (5, 1))
-    g1 = Gather(place, [qkv_view(*g) for g in groups], weight_send.at[pl.ds(0, 1)], g1_recv)
+    groups = (4, 5, 0, 1, 2, 3)
+    g1 = Gather(
+        place, [qkv_view(g) for g in groups], QKV_WAYS, weight_send.at[pl.ds(0, 1)], g1_recv
+    )
     columns = ((0, 2816), (2816, 2816), (5632, 1280), (6912, 1280))
-    g2 = Gather(place, [out_view(*c) for c in columns], weight_send.at[pl.ds(1, 1)], g2_recv)
+    g2 = Gather(
+        place, [out_view(*c) for c in columns], OUT_WAYS, weight_send.at[pl.ds(1, 1)], g2_recv
+    )
     g1.begin()
 
     acc[...] = jnp.zeros_like(acc)
@@ -399,25 +430,26 @@
 
     def project(here):
         for i, o in here:
-            first, count = groups[i]
-            w = jnp.concatenate([wqkv[o, g] for g in range(first, first + count)], axis=1)
-            acc[:, first * HD : (first + count) * HD] += nn(xn[o], w)
+            g = groups[i]
+            acc[:, g * HD : (g + 1) * HD] += nn(xn[o], wqkv[o, g])
+
+    def qkv_step(t):
+        return g1.step((0, t), (1, t), (5, t - 1), (4, t - 2), (2, t - 3), (3, t - 3))
 
     hid_load.wait()
     normalize(hid, 0)
-    first_here = g1.step(0)
+    first_here = qkv_step(0)
     saved_load.wait()
     inv_src = normalize(src, ROWS)
     wout_load.wait()
     cot_load.wait()
-    first_here += g1.step(1)
+    first_here += qkv_step(1)
     project(first_here)
-    for k in range(2, STEPS):
-        if k == 5:
+    for t in range(2, STEPS):
+        if t == STEPS - 4:
             g2.begin()
-        project(g1.step(k))
-        if k >= 7:
-            g2.step(k - 7)
+        project(qkv_step(t))
+    g2.step(0)
 
     def rotated(t, g):
         u = acc[t * ROWS : (t + 1) * ROWS, g * HD : (g + 1) * HD]
@@ -544,14 +576,22 @@
             for dx in range(4):
                 kv_take(1, dx, x_rows)
 
-    g2.step(3)
+    project(qkv_step(STEPS))
+    g2.step(1)
     kv_step(0)
+    project(qkv_step(STEPS + 1))
+    g2.step(2)
+    project(qkv_step(STEPS + 2))
+    kv_step(1)
     for t in range(2):
         for h in range(QH):
             queries[t, h * HD : (h + 1) * HD, :] = rotated(t, h)
-    for k in range(1, 4):
-        g2.step(3 + k)
-        kv_step(k)
+    g2.step(3)
+    kv_step(2)
+    g2.step(4)
+    g2.step(5)
+    kv_step(3)
+    g2.step(6)
     pair_copy.wait_send()
     pltpu.make_async_remote_copy(
         src_ref=pair_kv.at[parity],
@@ -615,7 +655,16 @@
         return row_max * LOG2 + jnp.log2(total)
 
     log_total = attend(1, ((7,), (8,)))
-    attend(0, ((9,), ()))
+
+    def attend_early():
+        attend(0, ((), ()))
+
+    early = section == 0
+    pl.when(early)(attend_early)
+
+    for k in range(9, STEPS):
+        g2.step((0, k), (1, k))
+    g2.step((2, 9), (3, 9))
 
     next_copies = [
         pltpu.make_async_remote_copy(
@@ -649,13 +698,17 @@
 
     def mix_back(steps):
         def body(c, total):
-            at = pl.ds(pl.multiple_of(c * OUT_COLS, OUT_COLS), OUT_COLS)
-            return total + nt(cot[:, at], wout[:, :, at].reshape(QH * HD, OUT_COLS))
+            at = pl.ds(pl.multiple_of(c * MIX_COLS, MIX_COLS), MIX_COLS)
+            return total + nt(wout[:, :, at].reshape(QH * HD, MIX_COLS), cot[:, at])
 
         mixing[...] = lax.fori_loop(steps[0], steps[1], body, mixing[...])
 
     mixing[...] = jnp.zeros_like(mixing)
-    pl.when(not_last)(lambda: mix_back((0, OUT_STEPS)))
+    pl.when(from_grad)(lambda: mix_back((0, MIX_FIRST)))
+    for k in range(10, STEPS):
+        g2.step((2, k), (3, k))
+    pl.when(early)(lambda: output(range(OUT_STEPS)))
+    pl.when(from_grad)(lambda: mix_back((MIX_FIRST, MIX_STEPS)))
 
     zero_next = [
         pltpu.make_async_copy(
@@ -681,6 +734,7 @@
     pl.when(is_last)(each(zero_prev, "start"))
 
     def reward_rows():
+        mixed[0] = mixed[1]
         output(range(OUT_STEPS))
         measure_output()
         mean_square = jnp.sum(squares[...], axis=1, keepdims=True) * (1.0 / D)
@@ -703,7 +757,7 @@
         down8 = lax.broadcasted_iota(jnp.int32, (RESP, 128), 0)
         sign = jnp.zeros((RESP, 128), f32)
         for p in range(PAIRS):
-            won, lost = pairs[p, 0], pairs[p, 1]
+            won, lost = pairs[0, p], pairs[1, p]
             sign += jnp.where(lost == answer, (down8 == won).astype(f32), 0.0)
             sign -= jnp.where(won == answer, (down8 == lost).astype(f32), 0.0)
         pltpu.make_async_remote_copy(
@@ -757,20 +811,21 @@
             return carry
 
         lax.fori_loop(0, D // 128, body, 0)
-        mix_back((0, OUT_STEPS))
+        mix_back((0, MIX_STEPS))
 
     def no_rewards():
         cot[...] = jnp.zeros_like(cot)
 
     pl.when(jnp.logical_and(is_last, in_answer))(reward_rows)
-    pl.when(jnp.logical_and(is_last, in_prompt))(no_rewards)
-
-    d_mixed = mixing[...].astype(bf16)
-    dots = d_mixed.astype(f32) * mixed[1].astype(f32)
+    pl.when(last_prompt)(no_rewards)
+
     row_dots = []
     for h in range(QH):
-        dheads[h * HD : (h + 1) * HD, :] = d_mixed[:, h * HD : (h + 1) * HD]
-        row_dots.append(jnp.sum(dots[:, h * HD : (h + 1) * HD].T, axis=0, keepdims=True))
+        at = slice(h * HD, (h + 1) * HD)
+        d_head = mixing[at, :].T.astype(bf16)
+        dheads[at, :] = d_head
+        dots = d_head.astype(f32) * mixed[1, :, at].astype(f32)
+        row_dots.append(jnp.sum(dots.T, axis=0, keepdims=True))
     row_dots = jnp.concatenate(row_dots, axis=1)
 
     q = queries[1]
@@ -807,8 +862,6 @@
             pl.when(there != own)(to_summer(side, there).start)
         return d_query
 
-    d_query = lax.fori_loop(0, 8, back_chunk, jnp.zeros((HD, QH * ROWS), f32))
-    d_query = attend_back(PBLK // 2, d_query) * SCALE
     to_partner = pltpu.make_async_remote_copy(
         src_ref=pair_dkv.at[1 - parity],
         dst_ref=pair_landed,
@@ -817,13 +870,27 @@
         device_id=other(partner),
         device_id_type=pl.DeviceIdType.MESH,
     )
-    pl.when(in_answer)(to_partner.start)
-
-    for h in range(QH):
-        u = d_query[:, h * HD : (h + 1) * HD].T
-        back[:, h * HD : (h + 1) * HD] = (u * cos - pltpu.roll(u, HD // 2, 1) * sin).astype(bf16)
-
-    pl.when(not_last)(lambda: output(range(OUT_STEPS)))
+
+    def back_through_keys():
+        d_query = lax.fori_loop(0, 8, back_chunk, jnp.zeros((HD, QH * ROWS), f32))
+        d_query = attend_back(PBLK // 2, d_query) * SCALE
+        pl.when(in_answer)(to_partner.start)
+        for h in range(QH):
+            u = d_query[:, h * HD : (h + 1) * HD].T
+            u = u * cos - pltpu.roll(u, HD // 2, 1) * sin
+            back[:, h * HD : (h + 1) * HD] = u.astype(bf16)
+
+    def no_query():
+        back[:, 0:512] = jnp.zeros((ROWS, QH * HD), bf16)
+
+    pl.when(sends_keys)(back_through_keys)
+    pl.when(last_prompt)(no_query)
+
+    def output_late():
+        attend(0, ((), ()))
+        output(range(OUT_STEPS))
+
+    pl.when(section == 1)(output_late)
 
     def column_copy(side):
         return pltpu.make_async_remote_copy(
@@ -835,94 +902,172 @@
             device_id_type=pl.DeviceIdType.MESH,
         )
 
-    for side in range(2):
-
-        def add(j, total, side=side):
-            there = beside(j)
-            pltpu.make_async_remote_copy(
-                src_ref=dkv.at[side, there],
-                dst_ref=landed.at[there, side],
-                send_sem=rs_send.at[0],
-                recv_sem=rs_recv.at[there * 2 + side],
-                device_id=other(partner),
-                device_id_type=pl.DeviceIdType.MESH,
-            ).wait_recv()
-            return total + landed[there, side].astype(f32)
-
-        column[side] = lax.fori_loop(1, 8, add, dkv[side, own].astype(f32)).astype(bf16)
-        pl.when(z != side)(column_copy(side).start)
+    def sum_plane():
+        for side in range(2):
+
+            def add(j, total, side=side):
+                there = beside(j)
+                pltpu.make_async_remote_copy(
+                    src_ref=dkv.at[side, there],
+                    dst_ref=landed.at[there, side],
+                    send_sem=rs_send.at[0],
+                    recv_sem=rs_recv.at[there * 2 + side],
+                    device_id=other(partner),
+                    device_id_type=pl.DeviceIdType.MESH,
+                ).wait_recv()
+                return total + landed[there, side].astype(f32)
+
+            column[side] = lax.fori_loop(1, 8, add, dkv[side, own].astype(f32)).astype(bf16)
+            pl.when(z != side)(column_copy(side).start)
+
+    pl.when(sends_keys)(sum_plane)
 
     def keep(total):
         u = total[:, :HD]
         back[:, 512:640] = (u * cos - pltpu.roll(u, HD // 2, 1) * sin).astype(bf16)
         back[:, 640:768] = total[:, HD:].astype(bf16)
 
+    def add_column(there, total):
+        pltpu.make_async_remote_copy(
+            src_ref=column.at[0],
+            dst_ref=column_landed.at[there],
+            send_sem=column_send.at[0],
+            recv_sem=column_recv.at[there],
+            device_id=other(partner),
+            device_id_type=pl.DeviceIdType.MESH,
+        ).wait_recv()
+        return total + column_landed[there].astype(f32)
+
     def sum_prompt():
         def add(j, total):
-            there = lax.rem(z + j, 4)
-            pltpu.make_async_remote_copy(
-                src_ref=column.at[0],
-                dst_ref=column_landed.at[there],
-                send_sem=column_send.at[0],
-                recv_sem=column_recv.at[there],
-                device_id=other(partner),
-                device_id_type=pl.DeviceIdType.MESH,
-            ).wait_recv()
-            return total + column_landed[there].astype(f32)
+            return add_column(lax.rem(z + j, 4), total)
 
         keep(lax.fori_loop(1, 4, add, column[z].astype(f32)))
+
+    def sum_last_prompt():
+        keep(lax.fori_loop(2, 4, add_column, jnp.zeros((BLK, 2 * HD), f32)))
 
     def sum_answer():
         to_partner.wait_recv()
         keep(pair_dkv[parity].astype(f32) + pair_landed[...].astype(f32))
 
-    pl.when(in_prompt)(sum_prompt)
-    pl.when(in_answer)(sum_answer)
-
-    back_all = back[...]
-    along = jnp.sum(back_all.astype(f32) * acc[ROWS:, :], axis=1, keepdims=True)
-    along = along * (inv_src * inv_src) * (1.0 / D)
-    prev_copies = []
-    for c in range(BACK_STEPS):
-        at = pl.ds(c * BACK_COLS, BACK_COLS)
-        w = jnp.concatenate(
-            [wqkv[2 * c : 2 * c + 2, g].reshape(BACK_COLS, HD) for g in range(QKV // HD)], axis=1
-        )
-        u = nt(back_all, w) * gain[:, at]
-        grad[:, at] = (
-            cot[:, at].astype(f32) + inv_src * u - src[:, at].astype(f32) * along
-        ).astype(bf16)
-        prev_copies.append(
+    pl.when(jnp.logical_and(from_grad, in_prompt))(sum_prompt)
+    pl.when(last_prompt)(sum_last_prompt)
+    pl.when(jnp.logical_and(has_back, in_answer))(sum_answer)
+
+    def columns_at(c):
+        return pl.ds(c * BACK_COLS, BACK_COLS)
+
+    def grad_copy(c, target, send_sem):
+        return pltpu.make_async_remote_copy(
+            src_ref=grad.at[:, columns_at(c)],
+            dst_ref=pg_hbm.at[0, :, columns_at(c)],
+            send_sem=send_sem,
+            recv_sem=prev_recv.at[c],
+            device_id=target,
+            device_id_type=pl.DeviceIdType.MESH,
+        )
+
+    prev_copies = [
+        grad_copy(c, {"section": (section + 3) % 4}, prev_send.at[c]) for c in range(BACK_STEPS)
+    ]
+    first_relay, second_relay, third_relay = [], [], []
+    for i, c in enumerate(ROUND):
+        at = columns_at(c)
+        first_relay.append(
             pltpu.make_async_remote_copy(
                 src_ref=grad.at[:, at],
-                dst_ref=pg_hbm.at[0, :, at],
+                dst_ref=grad.at[:, at],
                 send_sem=prev_send.at[c],
-                recv_sem=prev_recv.at[c],
+                recv_sem=relay_recv.at[i],
+                device_id={"section": (section + 2) % 4, "seq": across_y},
+                device_id_type=pl.DeviceIdType.MESH,
+            )
+        )
+        second_relay.append(
+            pltpu.make_async_remote_copy(
+                src_ref=grad.at[:, at],
+                dst_ref=relay.at[i],
+                send_sem=prev_send.at[c],
+                recv_sem=relay_recv.at[i],
                 device_id={"section": (section + 3) % 4},
                 device_id_type=pl.DeviceIdType.MESH,
             )
         )
-        pl.when(section > 0)(prev_copies[-1].start)
+        third_relay.append(
+            pltpu.make_async_remote_copy(
+                src_ref=relay.at[i],
+                dst_ref=pg_hbm.at[0, :, at],
+                send_sem=relay_send.at[i],
+                recv_sem=prev_recv.at[c],
+                device_id={"section": (section + 2) % 4, "seq": across_y},
+                device_id_type=pl.DeviceIdType.MESH,
+            )
+        )
+
+    def back_through_norm():
+        back_all = back[...]
+        along = jnp.sum(back_all.astype(f32) * acc[ROWS:, :], axis=1, keepdims=True)
+        along = along * (inv_src * inv_src) * (1.0 / D)
+        for c in range(BACK_STEPS):
+            at = columns_at(c)
+            w = jnp.concatenate(
+                [wqkv[2 * c : 2 * c + 2, g].reshape(BACK_COLS, HD) for g in range(QKV // HD)],
+                axis=1,
+            )
+            u = nt(back_all, w) * gain[:, at]
+            grad[:, at] = (
+                cot[:, at].astype(f32) + inv_src * u - src[:, at].astype(f32) * along
+            ).astype(bf16)
+            if c in ROUND:
+                pl.when(section == 2)(first_relay[ROUND.index(c)].start)
+                pl.when(section != 2)(prev_copies[c].start)
+            else:
+                prev_copies[c].start()
+
+    def pass_on():
+        for arriving, leaving in zip(first_relay, second_relay):
+            arriving.wait_recv()
+            leaving.start()
+
+    def pass_on_last():
+        for arriving, leaving in zip(second_relay, third_relay):
+            arriving.wait_recv()
+            leaving.start()
+
+    pl.when(has_back)(back_through_norm)
+    pl.when(section == 2)(output_late)
+    pl.when(section == 0)(pass_on)
+    pl.when(is_last)(pass_on_last)
 
     g1.finish(wqkv.at[pl.ds(0, SEQ - 1)])
     g2.finish(wout.at[pl.ds(0, SEQ - 1)])
     pl.when(in_prompt)(each([along_z(dz) for dz in (1, 3, 2)], "wait_send"))
     for copy in kv_sent:
         copy.wait_send()
-    for side in range(2):
-
-        def sent_on(there, carry, side=side):
-            pl.when(there != own)(to_summer(side, there).wait_send)
-            return carry
-
-        lax.fori_loop(0, 8, sent_on, 0)
-        pl.when(z != side)(column_copy(side).wait_send)
-    pl.when(in_answer)(to_partner.wait_send)
+    def keys_sent():
+        for side in range(2):
+
+            def sent_on(there, carry, side=side):
+                pl.when(there != own)(to_summer(side, there).wait_send)
+                return carry
+
+            lax.fori_loop(0, 8, sent_on, 0)
+            pl.when(z != side)(column_copy(side).wait_send)
+        pl.when(in_answer)(to_partner.wait_send)
+
+    pl.when(sends_keys)(keys_sent)
     pl.when(not_last)(each(next_copies, "wait_send"))
     pl.when(section > 0)(each(next_copies, "wait_recv"))
     pl.when(section == 0)(each(zero_next, "wait"))
     pl.when(is_last)(each(zero_prev, "wait"))
-    pl.when(section > 0)(each(prev_copies, "wait_send"))
+    straight = [prev_copies[c] for c in range(BACK_STEPS) if c not in ROUND]
+    around = [prev_copies[c] for c in ROUND]
+    pl.when(has_back)(each(straight, "wait_send"))
+    pl.when(jnp.logical_and(has_back, section != 2))(each(around, "wait_send"))
+    pl.when(section == 2)(each(first_relay, "wait_send"))
+    pl.when(section == 0)(each(second_relay, "wait_send"))
+    pl.when(is_last)(each(third_relay, "wait_send"))
     pl.when(not_last)(each(prev_copies, "wait_recv"))
 
 
@@ -982,7 +1127,7 @@
             pltpu.VMEM((ROWS, D), bf16),
             pltpu.VMEM((ROWS, 128), f32),
             pltpu.VMEM((ROWS, 128), f32),
-            pltpu.VMEM((ROWS, QH * HD), f32),
+            pltpu.VMEM((QH * HD, ROWS), f32),
             pltpu.VMEM((QH * ROWS, HD), bf16),
             pltpu.VMEM((2, 8, BLK, 256), bf16),
             pltpu.VMEM((2, BLK, 256), bf16),
@@ -993,10 +1138,11 @@
             pltpu.VMEM((2, 8, 8, 128), f32),
             pltpu.VMEM((ROWS, QKV), bf16),
             pltpu.VMEM((ROWS, D), bf16),
+            pltpu.VMEM((len(ROUND), ROWS, BACK_COLS), bf16),
             pltpu.VMEM((ROWS, OUT_COLS), bf16),
             dma((10,)),
             dma((2,)),
-            dma((160,)),
+            dma((240,)),
             dma((160,)),
             dma((4,)),
             dma((2,)),
@@ -1014,6 +1160,8 @@
             dma((OUT_STEPS,)),
             dma((BACK_STEPS,)),
             dma((BACK_STEPS,)),
+            dma((len(ROUND),)),
+            dma((len(ROUND),)),
             dma((OUT_STEPS,)),
         ],
         compiler_params=pltpu.CompilerParams(
@@ -1025,7 +1173,7 @@
     )(
         block_table,
         resp_lengths,
-        pairs,
+        pairs.T,
         hidden_in,
         saved_hidden,
         grad_in,

time: 181 us -> 167 us (0.923)
  Pallas kernels: 173 us -> 162 us
    pallas_call x1, Pallas kernels: 173 us -> 162 us  [per_device(): pl.pallas_call(layer_kernel, out_shape=(out, out), in_specs=[smem] * 3 +...]
    unnamed x5 -> x4, local copies, waits for them, and re-layouts: 5.94 us -> 4.57 us
where the time goes in v3:
time: 167 us
  Pallas kernels  162 us (97%)
  local copies, waits for them, and re-layouts  4.57 us (3%)
    pallas_call x1, Pallas kernels, per_device(): pl.pallas_call(layer_kernel, out_shape=(out, out), in_specs=[smem] * 3 +...  162 us
    unnamed x4, local copies, waits for them, and re-layouts  4.57 us

profile of v3, /device:TPU:1, one launch (start us, length us, event | category | flops | bytes accessed | tf_op | source)
XLA Modules:
  0.0 167.1 jit_solution(17521208933139622552)
XLA Ops:
  0.6 161.9 %shard_map.167 = (bf16[1,128,8192]{2,1,0:T(8,128)(2,1)}, bf16[1,128,8192]{2,1,0:T(8,128)(2,1)}) custom-call(s32[16]{0:T(128)} %block_table.1, s32[8]{0:T(128)} %lengths.1, s32[2,28]{1,0:T(2,128)} %bitcast.3, bf16[1,128,8192]{2,1,0:T(8,128)(2,1)} %hid_hbm.1, bf16[1,128,8192]{2,1,0:T(8,128)(2,1)} %sav_hbm.1, bf16[1,128,8192]{2,1,0:T(8,128)(2,1)} %gin_hbm.1, ...), custom_call_target="tpu_custom_call" | custom-call | flops 12000000000 | bytes 12000000 | tf_op jit(solution)/shard_map/pallas_call | solution.py:1109
  162.6 0.0 copy-start
  162.6 3.2 %copy.20 = bf16[1,128,8192]{2,1,0:T(8,128)(2,1)} copy(bf16[1,128,8192]{2,1,0:T(8,128)(2,1)} %get-tuple-element.4) | data formatting | bytes 4194304
  165.8 0.0 copy-done
  165.8 1.3 copy.21
Async XLA Ops:
  162.6 3.3 %copy-start = (bf16[1,128,8192]{2,1,0:T(8,128)(2,1)S(1)}, bf16[1,128,8192]{2,1,0:T(8,128)(2,1)}, u32[]{:S(2)}) copy-start(bf16[1,128,8192]{2,1,0:T(8,128)(2,1)} %get-tuple-element.5) | copy-start | bytes 6291460

commit v4 on v3

--- a/solution.py
+++ b/solution.py
@@ -263,7 +263,6 @@
     back,
     grad,
     relay,
-    zero,
     load_sems,
     weight_send,
     g1_recv,
@@ -286,7 +285,6 @@
     prev_recv,
     relay_send,
     relay_recv,
-    zero_sems,
 ):
     place = Place()
     seq, z = place.seq, place.zs[0]
@@ -327,12 +325,6 @@
     cot_load = pltpu.make_async_copy(gin_hbm.at[0], cot, load_sems.at[9])
     for load in loads:
         load.start()
-    hid_load.start()
-    pl.when(not_last)(saved_load.start)
-    pl.when(is_last)(again_load.start)
-    wout_load.start()
-    cot_load.start()
-
     barrier = pltpu.get_barrier_semaphore()
 
     def greet(index):
@@ -375,6 +367,11 @@
     )
     for load in loads:
         load.wait()
+    hid_load.start()
+    pl.when(not_last)(saved_load.start)
+    pl.when(is_last)(again_load.start)
+    wout_load.start()
+    cot_load.start()
     pl.semaphore_wait(barrier, 13)
 
     def qkv_view(group):
@@ -404,7 +401,6 @@
     g1.begin()
 
     acc[...] = jnp.zeros_like(acc)
-    zero[...] = jnp.zeros_like(zero)
 
     def inverse_rms(buf):
         def body(i, total):
@@ -710,28 +706,12 @@
     pl.when(early)(lambda: output(range(OUT_STEPS)))
     pl.when(from_grad)(lambda: mix_back((MIX_FIRST, MIX_STEPS)))
 
-    zero_next = [
-        pltpu.make_async_copy(
-            zero, nh_hbm.at[0, :, pl.ds(c * OUT_COLS, OUT_COLS)], zero_sems.at[c]
-        )
-        for c in range(OUT_STEPS)
-    ]
-    zero_prev = [
-        pltpu.make_async_copy(
-            zero, pg_hbm.at[0, :, pl.ds(c * OUT_COLS, OUT_COLS)], zero_sems.at[c]
-        )
-        for c in range(OUT_STEPS)
-    ]
-
     def each(copies, what):
         def run():
             for copy in copies:
                 getattr(copy, what)()
 
         return run
-
-    pl.when(section == 0)(each(zero_next, "start"))
-    pl.when(is_last)(each(zero_prev, "start"))
 
     def reward_rows():
         mixed[0] = mixed[1]
@@ -872,7 +852,7 @@
     )
 
     def back_through_keys():
-        d_query = lax.fori_loop(0, 8, back_chunk, jnp.zeros((HD, QH * ROWS), f32))
+        d_query = lax.fori_loop(0, 8, back_chunk, jnp.zeros((HD, QH * ROWS), f32), unroll=2)
         d_query = attend_back(PBLK // 2, d_query) * SCALE
         pl.when(in_answer)(to_partner.start)
         for h in range(QH):
@@ -1059,8 +1039,6 @@
     pl.when(sends_keys)(keys_sent)
     pl.when(not_last)(each(next_copies, "wait_send"))
     pl.when(section > 0)(each(next_copies, "wait_recv"))
-    pl.when(section == 0)(each(zero_next, "wait"))
-    pl.when(is_last)(each(zero_prev, "wait"))
     straight = [prev_copies[c] for c in range(BACK_STEPS) if c not in ROUND]
     around = [prev_copies[c] for c in ROUND]
     pl.when(has_back)(each(straight, "wait_send"))
@@ -1106,7 +1084,7 @@
     smem = pl.BlockSpec(memory_space=pltpu.SMEM)
     dma = pltpu.SemaphoreType.DMA
     out = jax.ShapeDtypeStruct((1, ROWS, D), bf16)
-    return pl.pallas_call(
+    next_hidden, prev_grad = pl.pallas_call(
         layer_kernel,
         out_shape=(out, out),
         in_specs=[smem] * 3 + [any_spec] * 7 + [vmem] * 6,
@@ -1139,7 +1117,6 @@
             pltpu.VMEM((ROWS, QKV), bf16),
             pltpu.VMEM((ROWS, D), bf16),
             pltpu.VMEM((len(ROUND), ROWS, BACK_COLS), bf16),
-            pltpu.VMEM((ROWS, OUT_COLS), bf16),
             dma((10,)),
             dma((2,)),
             dma((240,)),
@@ -1162,7 +1139,6 @@
             dma((BACK_STEPS,)),
             dma((len(ROUND),)),
             dma((len(ROUND),)),
-            dma((OUT_STEPS,)),
         ],
         compiler_params=pltpu.CompilerParams(
             collective_id=0, has_side_effects=True, vmem_limit_bytes=60 * 1024 * 1024
@@ -1185,6 +1161,12 @@
         head.reshape(D // 128, 128),
         *angle_tables(),
     )
+    section = lax.axis_index("section")
+    nothing = jnp.zeros((), bf16)
+    return (
+        jnp.where(section == 0, nothing, next_hidden),
+        jnp.where(section == SECTIONS - 1, nothing, prev_grad),
+    )
 
 
 def solution(mesh):

time: 167 us -> 167 us (level)
  local copies, waits for them, and re-layouts: 4.57 us -> 0 us
  other arithmetic: 0 us -> 4.52 us
    unnamed x4 -> x0, local copies, waits for them, and re-layouts: 4.57 us -> none
    select_n x0 -> x1, other arithmetic: none -> 4.52 us  [per_device(): jnp.where(section == SECTIONS - 1, nothing, prev_grad)]
where the time goes in v4:
time: 167 us
  Pallas kernels  162 us (97%)
  other arithmetic  4.52 us (3%)
    pallas_call x1, Pallas kernels, per_device(): pl.pallas_call(layer_kernel, out_shape=(out, out), in_specs=[smem] * 3 +...  162 us
    select_n x1, other arithmetic, per_device(): jnp.where(section == SECTIONS - 1, nothing, prev_grad)  4.52 us

profile of v4, /device:TPU:1, one launch (start us, length us, event | category | flops | bytes accessed | tf_op | source)
XLA Modules:
  0.0 166.7 jit_solution(5184503672354514581)
XLA Ops:
  0.6 161.6 %shard_map.167 = (bf16[1,128,8192]{2,1,0:T(8,128)(2,1)}, bf16[1,128,8192]{2,1,0:T(8,128)(2,1)}) custom-call(s32[16]{0:T(128)} %block_table.1, s32[8]{0:T(128)} %lengths.1, s32[2,28]{1,0:T(2,128)} %bitcast.3, bf16[1,128,8192]{2,1,0:T(8,128)(2,1)} %hid_hbm.1, bf16[1,128,8192]{2,1,0:T(8,128)(2,1)} %sav_hbm.1, bf16[1,128,8192]{2,1,0:T(8,128)(2,1)} %gin_hbm.1, ...), custom_call_target="tpu_custom_call" | custom-call | flops 12000000000 | bytes 12000000 | tf_op jit(solution)/shard_map/pallas_call | solution.py:1087
  162.2 4.5 %broadcast_select_fusion = (bf16[1,128,8192]{2,1,0:T(8,128)(2,1)}, bf16[1,128,8192]{2,1,0:T(8,128)(2,1)}) fusion(bf16[1,128,8192]{2,1,0:T(8,128)(2,1)} %get-tuple-element.5, pred[]{:T(512)S(6)} %eq.7, bf16[1,128,8192]{2,1,0:T(8,128)(2,1)} %get-tuple-element.4, pred[]{:T(512)S(6)} %eq.6), kind=kLoop, calls=%fused_computation | loop fusion | flops 2097152 | bytes 8388610 | tf_op jit(solution)/shard_map/jit(_where)/select_n | solution.py:1168

commit v5 on v4

--- a/solution.py
+++ b/solution.py
@@ -640,7 +640,7 @@
             jnp.zeros((HD, QH * ROWS), f32),
         )
         for start, then in zip((0, 4), between):
-            carry = lax.fori_loop(start, start + 4, chunk, carry)
+            carry = lax.fori_loop(start, start + 4, chunk, carry, unroll=2)
             for k in then:
                 g2.step(k)
         carry = chunk(PBLK // 2, carry)
@@ -697,7 +697,7 @@
             at = pl.ds(pl.multiple_of(c * MIX_COLS, MIX_COLS), MIX_COLS)
             return total + nt(wout[:, :, at].reshape(QH * HD, MIX_COLS), cot[:, at])
 
-        mixing[...] = lax.fori_loop(steps[0], steps[1], body, mixing[...])
+        mixing[...] = lax.fori_loop(steps[0], steps[1], body, mixing[...], unroll=True)
 
     mixing[...] = jnp.zeros_like(mixing)
     pl.when(from_grad)(lambda: mix_back((0, MIX_FIRST)))

time: 167 us -> 164 us (0.982)
  Pallas kernels: 162 us -> 159 us
    pallas_call x1, Pallas kernels: 162 us -> 159 us  [per_device(): pl.pallas_call(layer_kernel, out_shape=(out, out), in_specs=[smem] * 3 +...]
where the time goes in v5:
time: 164 us
  Pallas kernels  159 us (97%)
  other arithmetic  4.52 us (3%)
    pallas_call x1, Pallas kernels, per_device(): pl.pallas_call(layer_kernel, out_shape=(out, out), in_specs=[smem] * 3 +...  159 us
    select_n x1, other arithmetic, per_device(): jnp.where(section == SECTIONS - 1, nothing, prev_grad)  4.52 us

profile of v5, /device:TPU:1, one launch (start us, length us, event | category | flops | bytes accessed | tf_op | source)
XLA Modules:
  0.0 163.8 jit_solution(461688195931165472)
XLA Ops:
  0.6 158.6 %shard_map.167 = (bf16[1,128,8192]{2,1,0:T(8,128)(2,1)}, bf16[1,128,8192]{2,1,0:T(8,128)(2,1)}) custom-call(s32[16]{0:T(128)} %block_table.1, s32[8]{0:T(128)} %lengths.1, s32[2,28]{1,0:T(2,128)} %bitcast.3, bf16[1,128,8192]{2,1,0:T(8,128)(2,1)} %hid_hbm.1, bf16[1,128,8192]{2,1,0:T(8,128)(2,1)} %sav_hbm.1, bf16[1,128,8192]{2,1,0:T(8,128)(2,1)} %gin_hbm.1, ...), custom_call_target="tpu_custom_call" | custom-call | flops 12000000000 | bytes 12000000 | tf_op jit(solution)/shard_map/pallas_call | solution.py:1087
  159.3 4.5 %broadcast_select_fusion = (bf16[1,128,8192]{2,1,0:T(8,128)(2,1)}, bf16[1,128,8192]{2,1,0:T(8,128)(2,1)}) fusion(bf16[1,128,8192]{2,1,0:T(8,128)(2,1)} %get-tuple-element.5, pred[]{:T(512)S(6)} %eq.7, bf16[1,128,8192]{2,1,0:T(8,128)(2,1)} %get-tuple-element.4, pred[]{:T(512)S(6)} %eq.6), kind=kLoop, calls=%fused_computation | loop fusion | flops 2097152 | bytes 8388610 | tf_op jit(solution)/shard_map/jit(_where)/select_n | solution.py:1168
